TPU v7x, 256 devices: a whole 4x4x8 slice. The times are simulated.
256 devices in a mesh: gx: 128 (over z, x_lo, y, core), gz: 2 (over x_hi).
Axes of the slice: x: 4 (x_hi: 2, x_lo: 2; x = x_hi * 2 + x_lo), y: 4, z: 8, core: 2. Of those that a mesh axis runs over, the one named last changes fastest.
Arguments:
- queries: bfloat16 [65536, 1024], P(('gx', 'gz')), may hold values from -8 to 8
- key_rows: bfloat16 [65536, 1024], P(('gx', 'gz')), may hold values from -8 to 8
- value_rows: bfloat16 [65536, 1024], P(('gx', 'gz')), may hold values from -6 to 6
- grad_out: bfloat16 [65536, 1024], P(('gx', 'gz')), may hold values from -6 to 6
- pattern: int32 [512, 6, 2], P(('gx', 'gz')), may hold values from 0 to 1, as said below
Outputs:
- attended: bfloat16 [65536, 1024], P(('gx', 'gz'))
- grad_query: bfloat16 [65536, 1024], P(('gx', 'gz'))
- grad_key: bfloat16 [65536, 1024], P(('gx', 'gz'))
- grad_value: bfloat16 [65536, 1024], P(('gx', 'gz'))
Inputs may be any that keep to these rules, and one draw needn't show every extreme that they name: pattern[g, r, kb].
All inputs are finite; a program needn't handle non-finite values.
Results may differ from a plain program's by a relative error of at most 0.028.
Values may be sent and summed in bfloat16 or wider, within the bound.
No kernel may reach another device: no remote copies, remote signals or barrier semaphores. Data moves between devices by JAX's collectives and lax.ppermute only.
A program may use at most 128 MiB of HBM per device.

v0:
```python
import jax
import jax.numpy as jnp
from jax import lax
from jax.sharding import PartitionSpec as P

H = 16
HD = 64
BT = 128
NSRC = 6
QB = 2


def from_partner(x, axis, apart):
    return lax.ppermute(x, axis, [(i, i ^ 1 << apart) for i in range(lax.axis_size(axis))])


def shifted(x, axis, by):
    peers = lax.axis_size(axis)
    return lax.ppermute(x, axis, [(i, (i + by) % peers) for i in range(peers)])


def pair_scores(left, right):
    return jnp.einsum("tjd,kjd->jtk", left, right, preferred_element_type=jnp.float32)


def weigh(weights, right):
    return jnp.einsum("jtk,kjd->tjd", weights, right, preferred_element_type=jnp.float32)


def spread(weights, right):
    return jnp.einsum("jtk,tjd->kjd", weights, right, preferred_element_type=jnp.float32)


def local(queries, key_rows, value_rows, grad_out, pattern):
    tok_rows, features = queries.shape
    reach = lax.axis_size("gx") // 4
    key_value = jnp.stack([key_rows, value_rows])
    partner = from_partner(key_value, "gz", 0)
    slab_below, slab_above = [shifted(key_value, "gx", step_by) for step_by in (1, -1)]
    far_below, far_above = [shifted(key_value, "gx", step_by) for step_by in (reach, -reach)]
    sources = jnp.stack([key_value, partner, slab_below, slab_above, far_below, far_above])
    own_block = (jnp.arange(NSRC)[None, :, None] == 0) & (
        jnp.arange(QB)[:, None, None] == jnp.arange(QB)[None, None, :]
    )
    allowed = (pattern == 1) | own_block
    small = allowed.reshape(QB, NSRC * QB)
    mask = jnp.broadcast_to(small[:, None, :, None], (QB, BT, NSRC * QB, BT)).reshape(
        tok_rows, NSRC * tok_rows
    )
    scale = HD ** (-0.5)

    def block_of(array, index):
        return array[:, :, index * tok_rows : (index + 1) * tok_rows]

    def square_all(left, rights):
        return jnp.concatenate([pair_scores(left, rights[index]) for index in range(NSRC)], axis=2)

    def rows_all(weights, rights):
        return sum((weigh(block_of(weights, index), rights[index]) for index in range(NSRC)))

    def terms_all(weights, left):
        return jnp.stack([spread(block_of(weights, index), left) for index in range(NSRC)])

    group_cols = 2 * HD

    def group_pass(group):
        start = group * group_cols

        def column_cut(array):
            return lax.dynamic_slice_in_dim(array, start, group_cols, array.ndim - 1)

        query_part = column_cut(queries).reshape(tok_rows, 2, HD)
        grad_part = column_cut(grad_out).reshape(tok_rows, 2, HD)
        source_part = column_cut(sources)
        key_parts = source_part[:, 0].reshape(NSRC, tok_rows, 2, HD)
        value_parts = source_part[:, 1].reshape(NSRC, tok_rows, 2, HD)
        scores = square_all(query_part, key_parts) * scale
        masked = jnp.where(mask[None], scores, -jnp.inf)
        peak = jnp.max(masked, axis=2, keepdims=True)
        expo = jnp.exp(masked - peak)
        probs = expo / jnp.sum(expo, axis=2, keepdims=True)
        probs_low = probs.astype(jnp.bfloat16)
        output = rows_all(probs_low, value_parts)
        out_low = output.astype(jnp.bfloat16)
        delta = jnp.sum(grad_part.astype(jnp.float32) * out_low.astype(jnp.float32), axis=2).T[
            :, :, None
        ]
        dprobs = square_all(grad_part, value_parts)
        dscores_low = (probs * (dprobs - delta)).astype(jnp.bfloat16)
        query_grad = rows_all(dscores_low, key_parts) * scale
        key_terms = terms_all(dscores_low, query_part) * scale
        value_terms = terms_all(probs_low, grad_part)
        return (
            out_low.reshape(tok_rows, group_cols),
            query_grad.reshape(tok_rows, group_cols),
            key_terms.astype(jnp.bfloat16).reshape(NSRC, tok_rows, group_cols),
            value_terms.astype(jnp.bfloat16).reshape(NSRC, tok_rows, group_cols),
        )

    out_groups, query_groups, key_groups, value_groups = lax.map(
        group_pass, jnp.arange(H // 2, dtype=jnp.int32)
    )

    def join_groups(array):
        moved = jnp.moveaxis(array, 0, -2)
        return moved.reshape(moved.shape[:-2] + (features,))

    attended = join_groups(out_groups)
    grad_query = join_groups(query_groups).astype(jnp.bfloat16)
    terms = jnp.stack([join_groups(key_groups), join_groups(value_groups)], axis=1)
    total = terms[0].astype(jnp.float32) + from_partner(terms[1], "gz", 0).astype(jnp.float32)
    for index, step_by in ((2, -1), (3, 1), (4, -reach), (5, reach)):
        total = total + shifted(terms[index], "gx", step_by).astype(jnp.float32)
    return (attended, grad_query, total[0].astype(jnp.bfloat16), total[1].astype(jnp.bfloat16))


def solution(mesh):
    placed = (
        P(("gx", "gz"), None),
        P(("gx", "gz"), None),
        P(("gx", "gz"), None),
        P(("gx", "gz"), None),
        P(("gx", "gz"), None, None),
    )
    return jax.shard_map(
        local,
        mesh=mesh,
        in_specs=placed,
        out_specs=(
            P(("gx", "gz"), None),
            P(("gx", "gz"), None),
            P(("gx", "gz"), None),
            P(("gx", "gz"), None),
        ),
        check_vma=False,
    )
```

profile of v0, /device:TPU:32, one launch (start us, length us, event | category | flops | bytes accessed | tf_op | source)
XLA Modules:
  0.0 432.6 jit_solution(10611856254251143453)
XLA Ops:
  3.3 3.1 collective-permute-start
  6.4 4.8 %collective-permute-start.2 = (bf16[2,256,1024]{1,2,0:T(8,128)(2,1)S(1)}, bf16[2,256,1024]{1,2,0:T(8,128)(2,1)}, u32[]{:S(2)}, u32[]{:S(2)}) collective-permute-start(bf16[2,256,1024]{1,2,0:T(8,128)(2,1)S(1)} %pad_maximum_fusion), channel_id=1, source_target_pairs={{0,254},{2,0},{4,2},{6,4},{8,6},{10,8},{12,10},{14,12},{16,14},{18... | collective-permute-start | bytes 3145736 | tf_op jit(solution)/shard_map/ppermute | solution.py:19
  11.1 3.3 collective-permute-start.3
  14.4 2.1 collective-permute-start.4
  16.9 20.8 %collective-permute-done = bf16[2,256,1024]{1,2,0:T(8,128)(2,1)} collective-permute-done((bf16[2,256,1024]{1,2,0:T(8,128)(2,1)S(1)}, bf16[2,256,1024]{1,2,0:T(8,128)(2,1)}, u32[]{:S(2)}, u32[]{:S(2)}) %collective-permute-start) | collective-permute-done | bytes 1048608 | tf_op jit(solution)/shard_map/ppermute | solution.py:14
  39.0 1.3 bitcast_dynamic-update-slice_fusion.3
  40.3 2.2 collective-permute-done.2
  43.9 15.5 %collective-permute-done.3 = bf16[2,256,1024]{1,2,0:T(8,128)(2,1)} collective-permute-done((bf16[2,256,1024]{1,2,0:T(8,128)(2,1)S(1)}, bf16[2,256,1024]{1,2,0:T(8,128)(2,1)}, u32[]{:S(2)}, u32[]{:S(2)}) %collective-permute-start.3) | collective-permute-done | bytes 1048608 | tf_op jit(solution)/shard_map/ppermute | solution.py:19
  61.3 2.6 copy-done.10
  63.9 275.0 %while.17 = (s32[]{:T(128)}, bf16[8,256,128]{1,2,0:T(8,128)(2,1)}, bf16[8,256,128]{1,2,0:T(8,128)(2,1)}, bf16[8,6,256,128]{2,3,1,0:T(8,128)(2,1)}, bf16[8,6,256,...) while((s32[]{:T(128)}, bf16[8,256,128]{1,2,0:T(8,128)(2,1)}, ...), condition=%wide.region_4.5_spmd.clone, body=%wide.region_0.4_spmd.clone.sunk | while | flops 612992000 | bytes 50276996 | solution.py:100
  65.2 2.0 constant_dynamic-slice_fusion.17
  74.0 1.5 constant_dynamic-slice_fusion.19
  76.4 2.0 convolution_dynamic-update-slice_fusion.30
  84.9 2.2 copy.115
  87.1 3.1 fusion.255
  99.5 2.0 constant_dynamic-slice_fusion.17
  108.3 1.5 constant_dynamic-slice_fusion.19
  110.8 2.0 convolution_dynamic-update-slice_fusion.30
  119.2 2.2 copy.115
  121.5 3.1 fusion.255
  133.9 2.0 constant_dynamic-slice_fusion.17
  142.7 1.5 constant_dynamic-slice_fusion.19
  145.2 2.0 convolution_dynamic-update-slice_fusion.30
  153.6 2.2 copy.115
  155.9 3.1 fusion.255
  168.3 2.0 constant_dynamic-slice_fusion.17
  177.1 1.5 constant_dynamic-slice_fusion.19
  179.5 2.0 convolution_dynamic-update-slice_fusion.30
  188.0 2.2 copy.115
  190.2 3.1 fusion.255
  202.7 2.0 constant_dynamic-slice_fusion.17
  211.5 1.5 constant_dynamic-slice_fusion.19
  213.9 2.0 convolution_dynamic-update-slice_fusion.30
  222.4 2.2 copy.115
  224.6 3.1 fusion.255
  237.1 2.0 constant_dynamic-slice_fusion.17
  245.9 1.5 constant_dynamic-slice_fusion.19
  248.3 2.0 convolution_dynamic-update-slice_fusion.30
  256.8 2.2 copy.115
  259.0 3.1 fusion.255
  271.4 2.0 constant_dynamic-slice_fusion.17
  280.2 1.5 constant_dynamic-slice_fusion.19
  282.7 2.0 convolution_dynamic-update-slice_fusion.30
  291.1 2.2 copy.115
  293.4 3.1 fusion.255
  305.8 2.0 constant_dynamic-slice_fusion.17
  314.6 1.5 constant_dynamic-slice_fusion.19
  317.1 2.0 convolution_dynamic-update-slice_fusion.30
  325.5 2.2 copy.115
  327.8 3.1 fusion.255
  339.0 3.6 copy.75
  342.6 3.4 stack_reshape.6
  346.0 4.3 constant_dynamic-update-slice_fusion.16
  350.3 3.4 copy.76
  353.7 4.1 stack_reshape.7
  357.8 1.9 constant_dynamic-update-slice_fusion.15
  359.7 5.0 %slice_bitcast_fusion.4 = (bf16[2,256,1024]{2,1,0:T(8,128)(2,1)S(1)}, bf16[2,256,1024]{2,1,0:T(8,128)(2,1)}, bf16[2,256,1024]{2,1,0:T(8,128)(2,1)}, bf16[2,256,1024]{2,1,0:T(8,128)(2,1)}, bf16[2,256,1024]{2,1,0:T(8,128)(2,1)}) fusion(bf16[6,2,256,1024]{3,2,1,0:T(8,128)(2,1)} %constant_dynamic-update-slice_fusion.15), kind=kLoop, calls=%fused_computation.119 | loop fusion | bytes 10485760 | tf_op jit(solution)/shard_map/squeeze | solution.py:111
  364.7 13.8 %collective-permute-start.9 = (bf16[2,256,1024]{2,1,0:T(8,128)(2,1)}, bf16[2,256,1024]{2,1,0:T(8,128)(2,1)S(1)}, u32[]{:S(2)}, u32[]{:S(2)}) collective-permute-start(bf16[2,256,1024]{2,1,0:T(8,128)(2,1)} %get-tuple-element.147), channel_id=1, source_target_pairs={{0,64},{2,66},{4,68},{6,70},{8,72},{10,74},{12,76},{14,78},{16,80}... | collective-permute-start | bytes 3145736 | tf_op jit(solution)/shard_map/ppermute | solution.py:19
  378.6 4.8 %collective-permute-start.6 = (bf16[2,256,1024]{2,1,0:T(8,128)(2,1)}, bf16[2,256,1024]{2,1,0:T(8,128)(2,1)}, u32[]{:S(2)}, u32[]{:S(2)}) collective-permute-start(bf16[2,256,1024]{2,1,0:T(8,128)(2,1)} %get-tuple-element.150), channel_id=1, source_target_pairs={{0,254},{2,0},{4,2},{6,4},{8,6},{10,8},{12,10},{14,12},{16,14},{18... | collective-permute-start | bytes 3145736 | tf_op jit(solution)/shard_map/ppermute | solution.py:19
  383.8 2.0 copy.101
  385.9 2.0 copy.102
  387.9 8.6 %collective-permute-done.9 = bf16[2,256,1024]{2,1,0:T(8,128)(2,1)S(1)} collective-permute-done((bf16[2,256,1024]{2,1,0:T(8,128)(2,1)}, bf16[2,256,1024]{2,1,0:T(8,128)(2,1)S(1)}, u32[]{:S(2)}, u32[]{:S(2)}) %collective-permute-start.9) | collective-permute-done | bytes 1048608 | tf_op jit(solution)/shard_map/ppermute | solution.py:19
  396.5 31.5 %collective-permute-done.7 = bf16[2,256,1024]{2,1,0:T(8,128)(2,1)} collective-permute-done((bf16[2,256,1024]{2,1,0:T(8,128)(2,1)}, bf16[2,256,1024]{2,1,0:T(8,128)(2,1)}, u32[]{:S(2)}, u32[]{:S(2)}) %collective-permute-start.7) | collective-permute-done | bytes 1048608 | tf_op jit(solution)/shard_map/ppermute | solution.py:19
  428.0 3.6 fusion.51
  (649 shorter events, 190.5 us)
Async XLA Ops:
  0.6 15.9 %copy-start.12 = (s32[2,6,2]{1,2,0:T(2,128)S(1)}, s32[2,6,2]{1,2,0:T(2,128)}, u32[]{:S(2)}) copy-start(s32[2,6,2]{1,2,0:T(2,128)} %param.11) | copy-start | bytes 292
  3.3 34.5 %collective-permute-start = (bf16[2,256,1024]{1,2,0:T(8,128)(2,1)S(1)}, bf16[2,256,1024]{1,2,0:T(8,128)(2,1)}, u32[]{:S(2)}, u32[]{:S(2)}) collective-permute-start(bf16[2,256,1024]{1,2,0:T(8,128)(2,1)S(1)} %pad_maximum_fusion), channel_id=1, source_target_pairs={{0,1},{1,0},{2,3},{3,2},{4,5},{5,4},{6,7},{7,6},{8,9},{9,8},{10,11... | collective-permute-start | bytes 3145736 | tf_op jit(solution)/shard_map/ppermute | solution.py:14
  6.4 32.7 %collective-permute-start.1 = (bf16[2,256,1024]{1,2,0:T(8,128)(2,1)S(1)}, bf16[2,256,1024]{1,2,0:T(8,128)(2,1)}, u32[]{:S(2)}, u32[]{:S(2)}) collective-permute-start(bf16[2,256,1024]{1,2,0:T(8,128)(2,1)S(1)} %pad_maximum_fusion), channel_id=1, source_target_pairs={{0,2},{2,4},{4,6},{6,8},{8,10},{10,12},{12,14},{14,16},{16,18},{18... | collective-permute-start | bytes 3145736 | tf_op jit(solution)/shard_map/ppermute | solution.py:19
  6.4 36.2 %collective-permute-start.2 = (bf16[2,256,1024]{1,2,0:T(8,128)(2,1)S(1)}, bf16[2,256,1024]{1,2,0:T(8,128)(2,1)}, u32[]{:S(2)}, u32[]{:S(2)}) collective-permute-start(bf16[2,256,1024]{1,2,0:T(8,128)(2,1)S(1)} %pad_maximum_fusion), channel_id=1, source_target_pairs={{0,254},{2,0},{4,2},{6,4},{8,6},{10,8},{12,10},{14,12},{16,14},{18... | collective-permute-start | bytes 3145736 | tf_op jit(solution)/shard_map/ppermute | solution.py:19
  11.1 48.2 %collective-permute-start.3 = (bf16[2,256,1024]{1,2,0:T(8,128)(2,1)S(1)}, bf16[2,256,1024]{1,2,0:T(8,128)(2,1)}, u32[]{:S(2)}, u32[]{:S(2)}) collective-permute-start(bf16[2,256,1024]{1,2,0:T(8,128)(2,1)S(1)} %pad_maximum_fusion), channel_id=1, source_target_pairs={{0,64},{2,66},{4,68},{6,70},{8,72},{10,74},{12,76},{14,78},{16,80}... | collective-permute-start | bytes 3145736 | tf_op jit(solution)/shard_map/ppermute | solution.py:19
  14.4 46.8 %collective-permute-start.4 = (bf16[2,256,1024]{1,2,0:T(8,128)(2,1)S(1)}, bf16[2,256,1024]{1,2,0:T(8,128)(2,1)S(1)}, u32[]{:S(2)}, u32[]{:S(2)}) collective-permute-start(bf16[2,256,1024]{1,2,0:T(8,128)(2,1)S(1)} %pad_maximum_fusion), channel_id=1, source_target_pairs={{0,192},{2,194},{4,196},{6,198},{8,200},{10,202},{12,204},{14,206}... | collective-permute-start | bytes 3145736 | tf_op jit(solution)/shard_map/ppermute | solution.py:19
  61.3 2.7 copy-start.10
  67.1 6.8 %copy-start.1 = (bf16[1,1,256,128]{2,3,1,0:T(8,128)(2,1)}, bf16[1,1,256,128]{2,3,1,0:T(8,128)(2,1)S(1)}, u32[]{:S(2)}) copy-start(bf16[1,1,256,128]{2,3,1,0:T(8,128)(2,1)S(1)} %get-tuple-element.240) | copy-start | bytes 196612 | tf_op jit(solution)/shard_map/while
  76.4 6.3 %copy-start.8 = (bf16[1,1,256,128]{2,3,1,0:T(8,128)(2,1)S(1)}, bf16[1,1,256,128]{2,3,1,0:T(8,128)(2,1)}, u32[]{:S(2)}) copy-start(bf16[1,1,256,128]{2,3,1,0:T(8,128)(2,1)} %get-tuple-element.245) | copy-start | bytes 196612 | tf_op jit(solution)/shard_map/while
  90.2 1.2 copy-start.5
  90.2 1.3 copy-start.4
  90.2 1.5 copy-start.3
  90.2 1.7 copy-start.2
  92.1 1.7 copy-start.9
  101.5 6.8 %copy-start.1 = (bf16[1,1,256,128]{2,3,1,0:T(8,128)(2,1)}, bf16[1,1,256,128]{2,3,1,0:T(8,128)(2,1)S(1)}, u32[]{:S(2)}) copy-start(bf16[1,1,256,128]{2,3,1,0:T(8,128)(2,1)S(1)} %get-tuple-element.240) | copy-start | bytes 196612 | tf_op jit(solution)/shard_map/while
  110.7 6.3 %copy-start.8 = (bf16[1,1,256,128]{2,3,1,0:T(8,128)(2,1)S(1)}, bf16[1,1,256,128]{2,3,1,0:T(8,128)(2,1)}, u32[]{:S(2)}) copy-start(bf16[1,1,256,128]{2,3,1,0:T(8,128)(2,1)} %get-tuple-element.245) | copy-start | bytes 196612 | tf_op jit(solution)/shard_map/while
  124.6 1.2 copy-start.5
  124.6 1.3 copy-start.4
  124.6 1.5 copy-start.3
  124.6 1.7 copy-start.2
  126.5 1.7 copy-start.9
  135.9 6.8 %copy-start.1 = (bf16[1,1,256,128]{2,3,1,0:T(8,128)(2,1)}, bf16[1,1,256,128]{2,3,1,0:T(8,128)(2,1)S(1)}, u32[]{:S(2)}) copy-start(bf16[1,1,256,128]{2,3,1,0:T(8,128)(2,1)S(1)} %get-tuple-element.240) | copy-start | bytes 196612 | tf_op jit(solution)/shard_map/while
  145.1 6.3 %copy-start.8 = (bf16[1,1,256,128]{2,3,1,0:T(8,128)(2,1)S(1)}, bf16[1,1,256,128]{2,3,1,0:T(8,128)(2,1)}, u32[]{:S(2)}) copy-start(bf16[1,1,256,128]{2,3,1,0:T(8,128)(2,1)} %get-tuple-element.245) | copy-start | bytes 196612 | tf_op jit(solution)/shard_map/while
  159.0 1.2 copy-start.5
  159.0 1.3 copy-start.4
  159.0 1.5 copy-start.3
  159.0 1.7 copy-start.2
  160.9 1.7 copy-start.9
  170.3 6.8 %copy-start.1 = (bf16[1,1,256,128]{2,3,1,0:T(8,128)(2,1)}, bf16[1,1,256,128]{2,3,1,0:T(8,128)(2,1)S(1)}, u32[]{:S(2)}) copy-start(bf16[1,1,256,128]{2,3,1,0:T(8,128)(2,1)S(1)} %get-tuple-element.240) | copy-start | bytes 196612 | tf_op jit(solution)/shard_map/while
  179.5 6.3 %copy-start.8 = (bf16[1,1,256,128]{2,3,1,0:T(8,128)(2,1)S(1)}, bf16[1,1,256,128]{2,3,1,0:T(8,128)(2,1)}, u32[]{:S(2)}) copy-start(bf16[1,1,256,128]{2,3,1,0:T(8,128)(2,1)} %get-tuple-element.245) | copy-start | bytes 196612 | tf_op jit(solution)/shard_map/while
  193.4 1.3 copy-start.4
  193.4 1.5 copy-start.3
  193.4 1.7 copy-start.2
  195.3 1.7 copy-start.9
  204.7 6.8 %copy-start.1 = (bf16[1,1,256,128]{2,3,1,0:T(8,128)(2,1)}, bf16[1,1,256,128]{2,3,1,0:T(8,128)(2,1)S(1)}, u32[]{:S(2)}) copy-start(bf16[1,1,256,128]{2,3,1,0:T(8,128)(2,1)S(1)} %get-tuple-element.240) | copy-start | bytes 196612 | tf_op jit(solution)/shard_map/while
  213.9 6.3 %copy-start.8 = (bf16[1,1,256,128]{2,3,1,0:T(8,128)(2,1)S(1)}, bf16[1,1,256,128]{2,3,1,0:T(8,128)(2,1)}, u32[]{:S(2)}) copy-start(bf16[1,1,256,128]{2,3,1,0:T(8,128)(2,1)} %get-tuple-element.245) | copy-start | bytes 196612 | tf_op jit(solution)/shard_map/while
  227.7 1.3 copy-start.4
  227.7 1.5 copy-start.3
  227.8 1.7 copy-start.2
  229.7 1.7 copy-start.9
  239.1 6.8 %copy-start.1 = (bf16[1,1,256,128]{2,3,1,0:T(8,128)(2,1)}, bf16[1,1,256,128]{2,3,1,0:T(8,128)(2,1)S(1)}, u32[]{:S(2)}) copy-start(bf16[1,1,256,128]{2,3,1,0:T(8,128)(2,1)S(1)} %get-tuple-element.240) | copy-start | bytes 196612 | tf_op jit(solution)/shard_map/while
  248.3 6.3 %copy-start.8 = (bf16[1,1,256,128]{2,3,1,0:T(8,128)(2,1)S(1)}, bf16[1,1,256,128]{2,3,1,0:T(8,128)(2,1)}, u32[]{:S(2)}) copy-start(bf16[1,1,256,128]{2,3,1,0:T(8,128)(2,1)} %get-tuple-element.245) | copy-start | bytes 196612 | tf_op jit(solution)/shard_map/while
  262.1 1.3 copy-start.4
  262.1 1.5 copy-start.3
  262.2 1.7 copy-start.2
  264.0 1.7 copy-start.9
  273.4 6.8 %copy-start.1 = (bf16[1,1,256,128]{2,3,1,0:T(8,128)(2,1)}, bf16[1,1,256,128]{2,3,1,0:T(8,128)(2,1)S(1)}, u32[]{:S(2)}) copy-start(bf16[1,1,256,128]{2,3,1,0:T(8,128)(2,1)S(1)} %get-tuple-element.240) | copy-start | bytes 196612 | tf_op jit(solution)/shard_map/while
  282.6 6.3 %copy-start.8 = (bf16[1,1,256,128]{2,3,1,0:T(8,128)(2,1)S(1)}, bf16[1,1,256,128]{2,3,1,0:T(8,128)(2,1)}, u32[]{:S(2)}) copy-start(bf16[1,1,256,128]{2,3,1,0:T(8,128)(2,1)} %get-tuple-element.245) | copy-start | bytes 196612 | tf_op jit(solution)/shard_map/while
  296.5 1.3 copy-start.4
  296.5 1.5 copy-start.3
  296.5 1.7 copy-start.2
  298.4 1.7 copy-start.9
  307.8 6.8 %copy-start.1 = (bf16[1,1,256,128]{2,3,1,0:T(8,128)(2,1)}, bf16[1,1,256,128]{2,3,1,0:T(8,128)(2,1)S(1)}, u32[]{:S(2)}) copy-start(bf16[1,1,256,128]{2,3,1,0:T(8,128)(2,1)S(1)} %get-tuple-element.240) | copy-start | bytes 196612 | tf_op jit(solution)/shard_map/while
  317.0 6.3 %copy-start.8 = (bf16[1,1,256,128]{2,3,1,0:T(8,128)(2,1)S(1)}, bf16[1,1,256,128]{2,3,1,0:T(8,128)(2,1)}, u32[]{:S(2)}) copy-start(bf16[1,1,256,128]{2,3,1,0:T(8,128)(2,1)} %get-tuple-element.245) | copy-start | bytes 196612 | tf_op jit(solution)/shard_map/while
  330.9 1.3 copy-start.4
  330.9 1.5 copy-start.3
  330.9 1.7 copy-start.2
  332.8 1.7 copy-start.9
  346.0 4.3 copy-start.11
  364.7 31.8 %collective-permute-start.9 = (bf16[2,256,1024]{2,1,0:T(8,128)(2,1)}, bf16[2,256,1024]{2,1,0:T(8,128)(2,1)S(1)}, u32[]{:S(2)}, u32[]{:S(2)}) collective-permute-start(bf16[2,256,1024]{2,1,0:T(8,128)(2,1)} %get-tuple-element.147), channel_id=1, source_target_pairs={{0,64},{2,66},{4,68},{6,70},{8,72},{10,74},{12,76},{14,78},{16,80}... | collective-permute-start | bytes 3145736 | tf_op jit(solution)/shard_map/ppermute | solution.py:19
  378.6 17.9 %collective-permute-start.8 = (bf16[2,256,1024]{2,1,0:T(8,128)(2,1)}, bf16[2,256,1024]{2,1,0:T(8,128)(2,1)S(1)}, u32[]{:S(2)}, u32[]{:S(2)}) collective-permute-start(bf16[2,256,1024]{2,1,0:T(8,128)(2,1)} %get-tuple-element.148), channel_id=1, source_target_pairs={{0,192},{2,194},{4,196},{6,198},{8,200},{10,202},{12,204},{14,206}... | collective-permute-start | bytes 3145736 | tf_op jit(solution)/shard_map/ppermute | solution.py:19
  378.6 49.4 %collective-permute-start.7 = (bf16[2,256,1024]{2,1,0:T(8,128)(2,1)}, bf16[2,256,1024]{2,1,0:T(8,128)(2,1)}, u32[]{:S(2)}, u32[]{:S(2)}) collective-permute-start(bf16[2,256,1024]{2,1,0:T(8,128)(2,1)} %get-tuple-element.149), channel_id=1, source_target_pairs={{0,2},{2,4},{4,6},{6,8},{8,10},{10,12},{12,14},{14,16},{16,18},{18... | collective-permute-start | bytes 3145736 | tf_op jit(solution)/shard_map/ppermute | solution.py:19
  378.6 49.4 %collective-permute-start.6 = (bf16[2,256,1024]{2,1,0:T(8,128)(2,1)}, bf16[2,256,1024]{2,1,0:T(8,128)(2,1)}, u32[]{:S(2)}, u32[]{:S(2)}) collective-permute-start(bf16[2,256,1024]{2,1,0:T(8,128)(2,1)} %get-tuple-element.150), channel_id=1, source_target_pairs={{0,254},{2,0},{4,2},{6,4},{8,6},{10,8},{12,10},{14,12},{16,14},{18... | collective-permute-start | bytes 3145736 | tf_op jit(solution)/shard_map/ppermute | solution.py:19
  383.3 44.7 %collective-permute-start.5 = (bf16[2,256,1024]{2,1,0:T(8,128)(2,1)S(1)}, bf16[2,256,1024]{2,1,0:T(8,128)(2,1)}, u32[]{:S(2)}, u32[]{:S(2)}) collective-permute-start(bf16[2,256,1024]{2,1,0:T(8,128)(2,1)S(1)} %get-tuple-element.146), channel_id=1, source_target_pairs={{0,1},{1,0},{2,3},{3,2},{4,5},{5,4},{6,7},{7,6},{8,9},{9,8},{10,11... | collective-permute-start | bytes 3145736 | tf_op jit(solution)/shard_map/ppermute | solution.py:14
  (29 other events, 27.4 us)
where the time goes:
time: 438 us; the launch traced here: 433 us
  matrix products  141 us (32%)
  local copies, waits for them, and re-layouts  129 us (29%)
  waiting for transfers between devices  79.2 us (18%)
  other arithmetic  42.5 us (10%)
  starting transfers between devices  32.4 us (7%)
  loops' own time  7.77 us (2%)
    dot_general x96, matrix products, pair_scores(): jnp.einsum('tjd,kjd->jtk', left, right, preferred_element_type=jnp.float32)  105 us
    ppermute x8, waiting for transfers between devices, shifted(): return lax.ppermute(x, axis, [(i, (i + by) % peers) for i in range(peers)])  58.4 us
    ppermute x8, starting transfers between devices, shifted(): return lax.ppermute(x, axis, [(i, (i + by) % peers) for i in range(peers)])  28.8 us
    dynamic_slice x32, local copies, waits for them, and re-layouts, column_cut(): return lax.dynamic_slice_in_dim(array, start, group_cols, array.ndim - 1)  27.1 us
    sub x8, other arithmetic, group_pass(): expo = jnp.exp(masked - peak)  24.8 us
    ppermute x2, waiting for transfers between devices, from_partner(): lax.ppermute(x, axis, [(i, i ^ 1 << apart) for i in range(lax.axis_size(a...  20.8 us
    dot_general x96, matrix products, spread(): jnp.einsum('jtk,tjd->kjd', weights, right, preferred_element_type=jnp.flo...  19.2 us
    broadcast_in_dim x8, local copies, waits for them, and re-layouts, group_pass(): masked = jnp.where(mask[None], scores, -jnp.inf)  17.7 us
  transfers between devices with their start and end apart: 10, of which 6 were waited for; matrix products, arithmetic and copies ran while one was open for 2% of the time, Pallas kernels for 0%

commit v1 on v0

v1 whole, which is shorter than its diff:
```python
import jax
import jax.numpy as jnp
from jax import lax
from jax.experimental import pallas as pl
from jax.experimental.pallas import tpu as pltpu
from jax.sharding import PartitionSpec as P

HD = 64
BT = 128
NSRC = 6
QB = 2
ROWS = QB * BT
PAIR = 2 * HD
F = 1024
PAIRS = F // PAIR
SCALE = HD**-0.5

bf16 = jnp.bfloat16
f32 = jnp.float32


def nt(a, b):
    return lax.dot_general(a, b, (((1,), (1,)), ((), ())), preferred_element_type=f32)


def nn(a, b):
    return lax.dot_general(a, b, (((1,), (0,)), ((), ())), preferred_element_type=f32)


def pick(x, head):
    lanes = lax.broadcasted_iota(jnp.int32, x.shape, 1)
    mine = (lanes < HD) if head == 0 else (lanes >= HD)
    return jnp.where(mine, x, jnp.zeros_like(x))


def merge(x0, x1):
    lanes = lax.broadcasted_iota(jnp.int32, (ROWS, PAIR), 1)
    return jnp.where(lanes < HD, x0, x1)


def source_cols(r):
    return slice(r * ROWS, (r + 1) * ROWS)


def probs_kernel(pattern, q_ref, grad_ref, *refs):
    k_refs = refs[:NSRC]
    p_ref, scaled_ref, inv_ref = refs[NSRC : NSRC + 3]
    dv_refs = refs[NSRC + 3 : 2 * NSRC + 3]
    s_ref = refs[2 * NSRC + 3]
    q = q_ref[...] * bf16(SCALE)
    grad = grad_ref[...].astype(f32)
    invs = []
    scaled = []
    for head in range(2):
        qh = pick(q, head)
        for r in range(NSRC):
            s = nt(qh, k_refs[r][...])
            for g in range(QB):
                rows = slice(g * BT, (g + 1) * BT)
                for kb in range(QB):
                    part = s[rows, kb * BT : (kb + 1) * BT]
                    if r != 0 or g != kb:
                        part = part + jnp.where(pattern[g, r, kb] == 1, 0.0, -jnp.inf)
                    first = r * ROWS + kb * BT
                    s_ref[rows, first : first + BT] = part
        s = s_ref[...]
        peak = jnp.max(s, axis=1, keepdims=True)
        expo = jnp.exp(s - peak)
        inv = 1.0 / jnp.sum(expo, axis=1, keepdims=True)
        p_ref[head] = expo.astype(bf16)
        invs.append(inv)
        scaled.append(pick((grad * inv).astype(bf16), head))
    inv_ref[...] = merge(invs[0], invs[1])
    scaled_ref[...] = scaled[0] + scaled[1]
    left0, left1 = scaled[0].T, scaled[1].T
    for r in range(NSRC):
        cols = source_cols(r)
        t = nn(left0, p_ref[0, :, cols]) + nn(left1, p_ref[1, :, cols])
        dv_refs[r][...] = t.T.astype(bf16)


def grads_kernel(q_ref, grad_ref, scaled_ref, inv_ref, p_ref, *refs):
    k_refs = refs[:NSRC]
    v_refs = refs[NSRC : 2 * NSRC]
    o_ref, dq_ref = refs[2 * NSRC : 2 * NSRC + 2]
    dk_refs = refs[2 * NSRC + 2 : 3 * NSRC + 2]
    ds_ref = refs[3 * NSRC + 2]
    q = q_ref[...] * bf16(SCALE)
    inv = inv_ref[...]
    acc = [None, None]
    for head in range(2):
        for r in range(NSRC):
            t = nn(p_ref[head, :, source_cols(r)], v_refs[r][...])
            acc[head] = t if r == 0 else acc[head] + t
    low = (merge(acc[0], acc[1]) * inv).astype(bf16)
    o_ref[...] = low
    prod = grad_ref[...].astype(f32) * low.astype(f32) * inv
    dq = [None, None]
    for head in range(2):
        delta = jnp.sum(pick(prod, head), axis=1, keepdims=True)
        scaled = pick(scaled_ref[...], head)
        for r in range(NSRC):
            cols = source_cols(r)
            dp = nt(scaled, v_refs[r][...])
            ds = (p_ref[head, :, cols].astype(f32) * (dp - delta)).astype(bf16)
            ds_ref[head, :, cols] = ds
            t = nn(ds, k_refs[r][...])
            dq[head] = t if r == 0 else dq[head] + t
    dq_ref[...] = (merge(dq[0], dq[1]) * SCALE).astype(bf16)
    left0, left1 = pick(q, 0).T, pick(q, 1).T
    for r in range(NSRC):
        cols = source_cols(r)
        t = nn(left0, ds_ref[0, :, cols]) + nn(left1, ds_ref[1, :, cols])
        dk_refs[r][...] = t.T.astype(bf16)


pair_block = pl.BlockSpec((ROWS, PAIR), lambda h: (0, h))
probs_block = pl.BlockSpec((2, ROWS, NSRC * ROWS), lambda h: (h, 0, 0))
tall = jax.ShapeDtypeStruct((ROWS, F), bf16)
PAIR_FLOPS = 2 * 2 * ROWS * NSRC * ROWS * HD


def probs_pass(pattern, queries, grad_out, keys):
    outs = pl.pallas_call(
        probs_kernel,
        grid=(PAIRS,),
        in_specs=[pl.BlockSpec(memory_space=pltpu.SMEM)] + [pair_block] * (2 + NSRC),
        out_specs=[probs_block] + [pair_block] * (2 + NSRC),
        out_shape=[
            jax.ShapeDtypeStruct((2 * PAIRS, ROWS, NSRC * ROWS), bf16),
            tall,
            jax.ShapeDtypeStruct((ROWS, F), f32),
        ]
        + [tall] * NSRC,
        scratch_shapes=[pltpu.VMEM((ROWS, NSRC * ROWS), f32)],
        compiler_params=pltpu.CompilerParams(vmem_limit_bytes=40 * 2**20),
        cost_estimate=pl.CostEstimate(
            flops=16 * PAIRS * PAIR_FLOPS, bytes_accessed=24 * 2**20, transcendentals=0
        ),
        name="probs_pass",
    )(pattern, queries, grad_out, *keys)
    return outs[0], outs[1], outs[2], outs[3:]


def grads_pass(queries, grad_out, scaled, inv, probs, keys, values):
    outs = pl.pallas_call(
        grads_kernel,
        grid=(PAIRS,),
        in_specs=[pair_block] * 4 + [probs_block] + [pair_block] * (2 * NSRC),
        out_specs=[pair_block] * (2 + NSRC),
        out_shape=[tall] * (2 + NSRC),
        scratch_shapes=[pltpu.VMEM((2, ROWS, NSRC * ROWS), bf16)],
        compiler_params=pltpu.CompilerParams(vmem_limit_bytes=40 * 2**20),
        cost_estimate=pl.CostEstimate(
            flops=24 * PAIRS * PAIR_FLOPS, bytes_accessed=24 * 2**20, transcendentals=0
        ),
        name="grads_pass",
    )(queries, grad_out, scaled, inv, probs, *keys, *values)
    return outs[0], outs[1], outs[2:]


def from_partner(x):
    return lax.ppermute(x, "gz", [(0, 1), (1, 0)])


def shifted(x, by):
    peers = lax.axis_size("gx")
    return lax.ppermute(x, "gx", [(i, (i + by) % peers) for i in range(peers)])


def gather(x):
    reach = lax.axis_size("gx") // 4
    far_below, far_above = shifted(x, reach), shifted(x, -reach)
    below, above = shifted(x, 1), shifted(x, -1)
    return [x, from_partner(x), below, above, far_below, far_above]


def give_back(terms):
    reach = lax.axis_size("gx") // 4
    far_below, far_above = shifted(terms[4], -reach), shifted(terms[5], reach)
    below, above = shifted(terms[2], -1), shifted(terms[3], 1)
    partner = from_partner(terms[1])
    total = terms[0].astype(f32)
    for part in (partner, below, above, far_below, far_above):
        total = total + part.astype(f32)
    return total.astype(bf16)


def local(queries, key_rows, value_rows, grad_out, pattern):
    keys = gather(key_rows)
    values = gather(value_rows)
    probs, scaled, inv, value_terms = probs_pass(pattern, queries, grad_out, keys)
    grad_value = give_back(value_terms)
    attended, grad_query, key_terms = grads_pass(
        queries, grad_out, scaled, inv, probs, keys, values
    )
    grad_key = give_back(key_terms)
    return attended, grad_query, grad_key, grad_value


def solution(mesh):
    rows = P(("gx", "gz"), None)
    return jax.shard_map(
        local,
        mesh=mesh,
        in_specs=(rows, rows, rows, rows, P(("gx", "gz"), None, None)),
        out_specs=(rows,) * 4,
        check_vma=False,
    )
```

time: 438 us -> 134 us (0.31)
  the two profiles are of different devices: /device:TPU:32 before, /device:TPU:59 now
where the time goes in v1:
time: 134 us; the launch traced here: 133 us
  waiting for transfers between devices  46.4 us (35%)
  starting transfers between devices  42.4 us (32%)
  Pallas kernels  37.1 us (28%)
  local copies, waits for them, and re-layouts  3.9 us (3%)
  other arithmetic  2.8 us (2%)
    ppermute x16, waiting for transfers between devices, shifted(): return lax.ppermute(x, 'gx', [(i, (i + by) % peers) for i in range(peers)])  36.1 us
    ppermute x16, starting transfers between devices, shifted(): return lax.ppermute(x, 'gx', [(i, (i + by) % peers) for i in range(peers)])  34.7 us
    pallas_call x1, Pallas kernels, grads_pass(): pl.pallas_call(grads_kernel, grid=(PAIRS,), in_specs=[pair_block] * 4 + [...  21.1 us
    pallas_call x1, Pallas kernels, probs_pass(): pl.pallas_call(probs_kernel, grid=(PAIRS,), in_specs=[pl.BlockSpec(memory...  15.9 us
    ppermute x4, waiting for transfers between devices, from_partner(): return lax.ppermute(x, 'gz', [(0, 1), (1, 0)])  10.3 us
    ppermute x4, starting transfers between devices, from_partner(): return lax.ppermute(x, 'gz', [(0, 1), (1, 0)])  7.71 us
    unnamed x11, local copies, waits for them, and re-layouts  3.9 us
    convert_element_type x2, other arithmetic, give_back(): return total.astype(bf16)  2.8 us
  transfers between devices with their start and end apart: 20, of which 7 were waited for; matrix products, arithmetic and copies ran while one was open for 2% of the time, Pallas kernels for 28%

profile of v1, /device:TPU:59, one launch (start us, length us, event | category | flops | bytes accessed | tf_op | source)
XLA Modules:
  0.0 133.3 jit_solution(1405496518549729513)
XLA Ops:
  0.6 1.9 %collective-permute-start = (bf16[256,1024]{1,0:T(8,128)(2,1)}, bf16[256,1024]{1,0:T(8,128)(2,1)S(1)}, u32[]{:S(2)}, u32[]{:S(2)}) collective-permute-start(bf16[256,1024]{1,0:T(8,128)(2,1)} %refs_0_.3), channel_id=1, source_target_pairs={{0,1},{1,0},{2,3},{3,2},{4,5},{5,4},{6,7},{7,6},{8,9},{9,8},{10,11... | collective-permute-start | bytes 1572872 | tf_op jit(solution)/shard_map/ppermute | solution.py:163
  2.6 3.0 %collective-permute-start.1 = (bf16[256,1024]{1,0:T(8,128)(2,1)}, bf16[256,1024]{1,0:T(8,128)(2,1)S(1)}, u32[]{:S(2)}, u32[]{:S(2)}) collective-permute-start(bf16[256,1024]{1,0:T(8,128)(2,1)} %refs_0_.3), channel_id=1, source_target_pairs={{0,2},{2,4},{4,6},{6,8},{8,10},{10,12},{12,14},{14,16},{16,18},{18... | collective-permute-start | bytes 1572872 | tf_op jit(solution)/shard_map/ppermute | solution.py:168
  5.6 0.0 collective-permute-start.2
  5.6 4.2 %collective-permute-start.3 = (bf16[256,1024]{1,0:T(8,128)(2,1)}, bf16[256,1024]{1,0:T(8,128)(2,1)S(1)}, u32[]{:S(2)}, u32[]{:S(2)}) collective-permute-start(bf16[256,1024]{1,0:T(8,128)(2,1)} %refs_0_.3), channel_id=1, source_target_pairs={{0,64},{2,66},{4,68},{6,70},{8,72},{10,74},{12,76},{14,78},{16,80}... | collective-permute-start | bytes 1572872 | tf_op jit(solution)/shard_map/ppermute | solution.py:168
  9.8 0.0 collective-permute-start.4
  9.8 0.8 copy.9.pattern
  10.6 10.3 %collective-permute-done.refs_1_ = bf16[256,1024]{1,0:T(8,128)(2,1)S(1)} collective-permute-done((bf16[256,1024]{1,0:T(8,128)(2,1)}, bf16[256,1024]{1,0:T(8,128)(2,1)S(1)}, u32[]{:S(2)}, u32[]{:S(2)}) %collective-permute-start) | collective-permute-done | bytes 524320 | tf_op jit(solution)/shard_map/ppermute | solution.py:163
  20.9 1.8 %collective-permute-start.5 = (bf16[256,1024]{1,0:T(8,128)(2,1)}, bf16[256,1024]{1,0:T(8,128)(2,1)S(1)}, u32[]{:S(2)}, u32[]{:S(2)}) collective-permute-start(bf16[256,1024]{1,0:T(8,128)(2,1)} %refs_6_.1), channel_id=1, source_target_pairs={{0,1},{1,0},{2,3},{3,2},{4,5},{5,4},{6,7},{7,6},{8,9},{9,8},{10,11... | collective-permute-start | bytes 1572872 | tf_op jit(solution)/shard_map/ppermute | solution.py:163
  22.7 0.0 collective-permute-done.1.refs_2_
  22.7 3.0 %collective-permute-start.6 = (bf16[256,1024]{1,0:T(8,128)(2,1)}, bf16[256,1024]{1,0:T(8,128)(2,1)S(1)}, u32[]{:S(2)}, u32[]{:S(2)}) collective-permute-start(bf16[256,1024]{1,0:T(8,128)(2,1)} %refs_6_.1), channel_id=1, source_target_pairs={{0,2},{2,4},{4,6},{6,8},{8,10},{10,12},{12,14},{14,16},{16,18},{18... | collective-permute-start | bytes 1572872 | tf_op jit(solution)/shard_map/ppermute | solution.py:168
  25.7 2.4 %collective-permute-done.2.refs_3_ = bf16[256,1024]{1,0:T(8,128)(2,1)S(1)} collective-permute-done((bf16[256,1024]{1,0:T(8,128)(2,1)}, bf16[256,1024]{1,0:T(8,128)(2,1)S(1)}, u32[]{:S(2)}, u32[]{:S(2)}) %collective-permute-start.2) | collective-permute-done | bytes 524320 | tf_op jit(solution)/shard_map/ppermute | solution.py:168
  28.1 0.0 collective-permute-start.7
  28.1 9.0 %collective-permute-done.3.refs_4_ = bf16[256,1024]{1,0:T(8,128)(2,1)S(1)} collective-permute-done((bf16[256,1024]{1,0:T(8,128)(2,1)}, bf16[256,1024]{1,0:T(8,128)(2,1)S(1)}, u32[]{:S(2)}, u32[]{:S(2)}) %collective-permute-start.3) | collective-permute-done | bytes 524320 | tf_op jit(solution)/shard_map/ppermute | solution.py:168
  37.1 3.1 %collective-permute-start.8 = (bf16[256,1024]{1,0:T(8,128)(2,1)}, bf16[256,1024]{1,0:T(8,128)(2,1)S(1)}, u32[]{:S(2)}, u32[]{:S(2)}) collective-permute-start(bf16[256,1024]{1,0:T(8,128)(2,1)} %refs_6_.1), channel_id=1, source_target_pairs={{0,64},{2,66},{4,68},{6,70},{8,72},{10,74},{12,76},{14,78},{16,80}... | collective-permute-start | bytes 1572872 | tf_op jit(solution)/shard_map/ppermute | solution.py:168
  40.1 0.0 collective-permute-done.4.refs_5_
  40.2 0.5 collective-permute-start.9
  40.7 0.0 copy-start
  40.7 1.0 copy-done
  41.7 0.0 copy-start.2
  41.7 1.0 copy-done.2
  42.7 0.0 copy-start.3
  42.7 1.0 copy-done.3
  43.8 0.0 copy-start.1
  43.8 0.0 copy-start.4
  43.8 15.9 %probs_pass.1 = (bf16[16,256,1536]{2,1,0:T(8,128)(2,1)}, bf16[256,1024]{1,0:T(8,128)(2,1)S(1)}, f32[256,1024]{1,0:T(8,128)S(1)}, bf16[256,1024]{1,0:T(8,128)(2,1...) custom-call(s32[2,6,2]{2,1,0:T(8,128)S(1)} %copy.9.pattern, ...), custom_call_target="tpu_custom_call" | custom-call | flops 12884901888 | bytes 25165824 | tf_op jit(solution)/shard_map/probs_pass/pallas_call | solution.py:124
  59.7 0.0 collective-permute-done.5.refs_7_
  59.7 1.4 %collective-permute-start.15 = (bf16[256,1024]{1,0:T(8,128)(2,1)S(1)}, bf16[256,1024]{1,0:T(8,128)(2,1)S(1)}, u32[]{:S(2)}, u32[]{:S(2)}) collective-permute-start(bf16[256,1024]{1,0:T(8,128)(2,1)S(1)} %get-tuple-element.33), channel_id=1, source_target_pairs={{0,1},{1,0},{2,3},{3,2},{4,5},{5,4},{6,7},{7,6},{8,9},{9,8},{10,11... | collective-permute-start | bytes 1572872 | tf_op jit(solution)/shard_map/ppermute | solution.py:163
  61.1 0.0 collective-permute-done.6.refs_8_
  61.1 0.0 collective-permute-start.16
  61.1 0.0 collective-permute-done.7.refs_9_
  61.1 7.4 %collective-permute-start.17 = (bf16[256,1024]{1,0:T(8,128)(2,1)S(1)}, bf16[256,1024]{1,0:T(8,128)(2,1)S(1)}, u32[]{:S(2)}, u32[]{:S(2)}) collective-permute-start(bf16[256,1024]{1,0:T(8,128)(2,1)S(1)} %get-tuple-element.35), channel_id=1, source_target_pairs={{0,2},{2,4},{4,6},{6,8},{8,10},{10,12},{12,14},{14,16},{16,18},{18... | collective-permute-start | bytes 1572872 | tf_op jit(solution)/shard_map/ppermute | solution.py:168
  68.6 0.0 collective-permute-done.8.refs_10_
  68.6 2.6 %collective-permute-start.18 = (bf16[256,1024]{1,0:T(8,128)(2,1)S(1)}, bf16[256,1024]{1,0:T(8,128)(2,1)S(1)}, u32[]{:S(2)}, u32[]{:S(2)}) collective-permute-start(bf16[256,1024]{1,0:T(8,128)(2,1)S(1)} %get-tuple-element.36), channel_id=1, source_target_pairs={{0,192},{2,194},{4,196},{6,198},{8,200},{10,202},{12,204},{14,206}... | collective-permute-start | bytes 1572872 | tf_op jit(solution)/shard_map/ppermute | solution.py:168
  71.2 0.0 collective-permute-done.9.refs_11_
  71.2 1.5 %collective-permute-start.19 = (bf16[256,1024]{1,0:T(8,128)(2,1)S(1)}, bf16[256,1024]{1,0:T(8,128)(2,1)S(1)}, u32[]{:S(2)}, u32[]{:S(2)}) collective-permute-start(bf16[256,1024]{1,0:T(8,128)(2,1)S(1)} %get-tuple-element.37), channel_id=1, source_target_pairs={{0,64},{2,66},{4,68},{6,70},{8,72},{10,74},{12,76},{14,78},{16,80}... | collective-permute-start | bytes 1572872 | tf_op jit(solution)/shard_map/ppermute | solution.py:168
  72.7 0.0 copy-done.1
  72.7 0.0 copy-done.4
  72.7 21.1 %grads_pass.1 = (bf16[256,1024]{1,0:T(8,128)(2,1)}, bf16[256,1024]{1,0:T(8,128)(2,1)}, bf16[256,1024]{1,0:T(8,128)(2,1)S(1)}, bf16[256,1024]{1,0:T(8,128)(2,1)S(...) custom-call(bf16[256,1024]{1,0:T(8,128)(2,1)S(1)} %copy-done.1, ...), custom_call_target="tpu_custom_call" | custom-call | flops 19327352832 | bytes 25165824 | tf_op jit(solution)/shard_map/grads_pass/pallas_call | solution.py:146
  93.8 0.0 collective-permute-done.15
  93.8 2.5 %collective-permute-start.10 = (bf16[256,1024]{1,0:T(8,128)(2,1)S(1)}, bf16[256,1024]{1,0:T(8,128)(2,1)S(1)}, u32[]{:S(2)}, u32[]{:S(2)}) collective-permute-start(bf16[256,1024]{1,0:T(8,128)(2,1)S(1)} %get-tuple-element.27), channel_id=1, source_target_pairs={{0,1},{1,0},{2,3},{3,2},{4,5},{5,4},{6,7},{7,6},{8,9},{9,8},{10,11... | collective-permute-start | bytes 1572872 | tf_op jit(solution)/shard_map/ppermute | solution.py:163
  96.4 0.0 collective-permute-done.16
  96.4 0.0 collective-permute-start.11
  96.4 0.0 collective-permute-done.17
  96.4 4.8 %collective-permute-start.12 = (bf16[256,1024]{1,0:T(8,128)(2,1)S(1)}, bf16[256,1024]{1,0:T(8,128)(2,1)S(1)}, u32[]{:S(2)}, u32[]{:S(2)}) collective-permute-start(bf16[256,1024]{1,0:T(8,128)(2,1)S(1)} %get-tuple-element.29), channel_id=1, source_target_pairs={{0,2},{2,4},{4,6},{6,8},{8,10},{10,12},{12,14},{14,16},{16,18},{18... | collective-permute-start | bytes 1572872 | tf_op jit(solution)/shard_map/ppermute | solution.py:168
  101.1 0.0 collective-permute-done.18
  101.1 3.0 %collective-permute-start.13 = (bf16[256,1024]{1,0:T(8,128)(2,1)S(1)}, bf16[256,1024]{1,0:T(8,128)(2,1)S(1)}, u32[]{:S(2)}, u32[]{:S(2)}) collective-permute-start(bf16[256,1024]{1,0:T(8,128)(2,1)S(1)} %get-tuple-element.30), channel_id=1, source_target_pairs={{0,192},{2,194},{4,196},{6,198},{8,200},{10,202},{12,204},{14,206}... | collective-permute-start | bytes 1572872 | tf_op jit(solution)/shard_map/ppermute | solution.py:168
  104.1 0.0 collective-permute-done.19
  104.2 1.6 %collective-permute-start.14 = (bf16[256,1024]{1,0:T(8,128)(2,1)S(1)}, bf16[256,1024]{1,0:T(8,128)(2,1)S(1)}, u32[]{:S(2)}, u32[]{:S(2)}) collective-permute-start(bf16[256,1024]{1,0:T(8,128)(2,1)S(1)} %get-tuple-element.31), channel_id=1, source_target_pairs={{0,64},{2,66},{4,68},{6,70},{8,72},{10,74},{12,76},{14,78},{16,80}... | collective-permute-start | bytes 1572872 | tf_op jit(solution)/shard_map/ppermute | solution.py:168
  105.8 1.4 %add_convert_fusion = bf16[256,1024]{1,0:T(8,128)(2,1)} fusion(bf16[256,1024]{1,0:T(8,128)(2,1)S(1)} %collective-permute-done.19, bf16[256,1024]{1,0:T(8,128)(2,1)S(1)} %collective-permute-done.18, bf16[256,1024]{1,0:T(8,128)(2,1)S(1)} %collective-permute-done.17, bf16[256,1024]{1,0:T(8,128)(2,1)S(1)} %collective-permute-done.16, ...), kind=kLoop, calls=%fused_computation | loop fusion | flops 3145728 | bytes 3670016 | tf_op jit(solution)/shard_map/convert_element_type | solution.py:186
  107.2 0.0 collective-permute-done.10
  107.2 9.5 %collective-permute-done.11 = bf16[256,1024]{1,0:T(8,128)(2,1)S(1)} collective-permute-done((bf16[256,1024]{1,0:T(8,128)(2,1)S(1)}, bf16[256,1024]{1,0:T(8,128)(2,1)S(1)}, u32[]{:S(2)}, u32[]{:S(2)}) %collective-permute-start.11) | collective-permute-done | bytes 524320 | tf_op jit(solution)/shard_map/ppermute | solution.py:168
  116.7 6.3 %collective-permute-done.12 = bf16[256,1024]{1,0:T(8,128)(2,1)S(1)} collective-permute-done((bf16[256,1024]{1,0:T(8,128)(2,1)S(1)}, bf16[256,1024]{1,0:T(8,128)(2,1)S(1)}, u32[]{:S(2)}, u32[]{:S(2)}) %collective-permute-start.12) | collective-permute-done | bytes 524320 | tf_op jit(solution)/shard_map/ppermute | solution.py:168
  123.0 1.3 collective-permute-done.13
  124.2 7.6 %collective-permute-done.14 = bf16[256,1024]{1,0:T(8,128)(2,1)S(1)} collective-permute-done((bf16[256,1024]{1,0:T(8,128)(2,1)S(1)}, bf16[256,1024]{1,0:T(8,128)(2,1)S(1)}, u32[]{:S(2)}, u32[]{:S(2)}) %collective-permute-start.14) | collective-permute-done | bytes 524320 | tf_op jit(solution)/shard_map/ppermute | solution.py:168
  131.9 1.4 %add_convert_fusion.1 = bf16[256,1024]{1,0:T(8,128)(2,1)} fusion(bf16[256,1024]{1,0:T(8,128)(2,1)S(1)} %collective-permute-done.14, bf16[256,1024]{1,0:T(8,128)(2,1)S(1)} %collective-permute-done.13, bf16[256,1024]{1,0:T(8,128)(2,1)S(1)} %collective-permute-done.12, bf16[256,1024]{1,0:T(8,128)(2,1)S(1)} %collective-permute-done.11, ...), kind=kLoop, calls=%fused_computation.1 | loop fusion | flops 3145728 | bytes 3670016 | tf_op jit(solution)/shard_map/convert_element_type | solution.py:186
Async XLA Ops:
  0.6 20.2 %collective-permute-start = (bf16[256,1024]{1,0:T(8,128)(2,1)}, bf16[256,1024]{1,0:T(8,128)(2,1)S(1)}, u32[]{:S(2)}, u32[]{:S(2)}) collective-permute-start(bf16[256,1024]{1,0:T(8,128)(2,1)} %refs_0_.3), channel_id=1, source_target_pairs={{0,1},{1,0},{2,3},{3,2},{4,5},{5,4},{6,7},{7,6},{8,9},{9,8},{10,11... | collective-permute-start | bytes 1572872 | tf_op jit(solution)/shard_map/ppermute | solution.py:163
  2.6 20.1 %collective-permute-start.1 = (bf16[256,1024]{1,0:T(8,128)(2,1)}, bf16[256,1024]{1,0:T(8,128)(2,1)S(1)}, u32[]{:S(2)}, u32[]{:S(2)}) collective-permute-start(bf16[256,1024]{1,0:T(8,128)(2,1)} %refs_0_.3), channel_id=1, source_target_pairs={{0,2},{2,4},{4,6},{6,8},{8,10},{10,12},{12,14},{14,16},{16,18},{18... | collective-permute-start | bytes 1572872 | tf_op jit(solution)/shard_map/ppermute | solution.py:168
  5.6 22.5 %collective-permute-start.2 = (bf16[256,1024]{1,0:T(8,128)(2,1)}, bf16[256,1024]{1,0:T(8,128)(2,1)S(1)}, u32[]{:S(2)}, u32[]{:S(2)}) collective-permute-start(bf16[256,1024]{1,0:T(8,128)(2,1)} %refs_0_.3), channel_id=1, source_target_pairs={{0,254},{2,0},{4,2},{6,4},{8,6},{10,8},{12,10},{14,12},{16,14},{18... | collective-permute-start | bytes 1572872 | tf_op jit(solution)/shard_map/ppermute | solution.py:168
  5.6 31.5 %collective-permute-start.3 = (bf16[256,1024]{1,0:T(8,128)(2,1)}, bf16[256,1024]{1,0:T(8,128)(2,1)S(1)}, u32[]{:S(2)}, u32[]{:S(2)}) collective-permute-start(bf16[256,1024]{1,0:T(8,128)(2,1)} %refs_0_.3), channel_id=1, source_target_pairs={{0,64},{2,66},{4,68},{6,70},{8,72},{10,74},{12,76},{14,78},{16,80}... | collective-permute-start | bytes 1572872 | tf_op jit(solution)/shard_map/ppermute | solution.py:168
  9.8 30.4 %collective-permute-start.4 = (bf16[256,1024]{1,0:T(8,128)(2,1)}, bf16[256,1024]{1,0:T(8,128)(2,1)S(1)}, u32[]{:S(2)}, u32[]{:S(2)}) collective-permute-start(bf16[256,1024]{1,0:T(8,128)(2,1)} %refs_0_.3), channel_id=1, source_target_pairs={{0,192},{2,194},{4,196},{6,198},{8,200},{10,202},{12,204},{14,206}... | collective-permute-start | bytes 1572872 | tf_op jit(solution)/shard_map/ppermute | solution.py:168
  20.9 38.9 %collective-permute-start.5 = (bf16[256,1024]{1,0:T(8,128)(2,1)}, bf16[256,1024]{1,0:T(8,128)(2,1)S(1)}, u32[]{:S(2)}, u32[]{:S(2)}) collective-permute-start(bf16[256,1024]{1,0:T(8,128)(2,1)} %refs_6_.1), channel_id=1, source_target_pairs={{0,1},{1,0},{2,3},{3,2},{4,5},{5,4},{6,7},{7,6},{8,9},{9,8},{10,11... | collective-permute-start | bytes 1572872 | tf_op jit(solution)/shard_map/ppermute | solution.py:163
  22.7 38.4 %collective-permute-start.6 = (bf16[256,1024]{1,0:T(8,128)(2,1)}, bf16[256,1024]{1,0:T(8,128)(2,1)S(1)}, u32[]{:S(2)}, u32[]{:S(2)}) collective-permute-start(bf16[256,1024]{1,0:T(8,128)(2,1)} %refs_6_.1), channel_id=1, source_target_pairs={{0,2},{2,4},{4,6},{6,8},{8,10},{10,12},{12,14},{14,16},{16,18},{18... | collective-permute-start | bytes 1572872 | tf_op jit(solution)/shard_map/ppermute | solution.py:168
  28.1 33.1 %collective-permute-start.7 = (bf16[256,1024]{1,0:T(8,128)(2,1)}, bf16[256,1024]{1,0:T(8,128)(2,1)S(1)}, u32[]{:S(2)}, u32[]{:S(2)}) collective-permute-start(bf16[256,1024]{1,0:T(8,128)(2,1)} %refs_6_.1), channel_id=1, source_target_pairs={{0,254},{2,0},{4,2},{6,4},{8,6},{10,8},{12,10},{14,12},{16,14},{18... | collective-permute-start | bytes 1572872 | tf_op jit(solution)/shard_map/ppermute | solution.py:168
  37.1 31.5 %collective-permute-start.8 = (bf16[256,1024]{1,0:T(8,128)(2,1)}, bf16[256,1024]{1,0:T(8,128)(2,1)S(1)}, u32[]{:S(2)}, u32[]{:S(2)}) collective-permute-start(bf16[256,1024]{1,0:T(8,128)(2,1)} %refs_6_.1), channel_id=1, source_target_pairs={{0,64},{2,66},{4,68},{6,70},{8,72},{10,74},{12,76},{14,78},{16,80}... | collective-permute-start | bytes 1572872 | tf_op jit(solution)/shard_map/ppermute | solution.py:168
  40.2 31.1 %collective-permute-start.9 = (bf16[256,1024]{1,0:T(8,128)(2,1)}, bf16[256,1024]{1,0:T(8,128)(2,1)S(1)}, u32[]{:S(2)}, u32[]{:S(2)}) collective-permute-start(bf16[256,1024]{1,0:T(8,128)(2,1)} %refs_6_.1), channel_id=1, source_target_pairs={{0,192},{2,194},{4,196},{6,198},{8,200},{10,202},{12,204},{14,206}... | collective-permute-start | bytes 1572872 | tf_op jit(solution)/shard_map/ppermute | solution.py:168
  40.7 1.0 copy-start
  41.7 1.0 copy-start.2
  42.7 1.0 copy-start.3
  43.8 28.9 %copy-start.1 = (bf16[256,1024]{1,0:T(8,128)(2,1)S(1)}, bf16[256,1024]{1,0:T(8,128)(2,1)}, u32[]{:S(2)}) copy-start(bf16[256,1024]{1,0:T(8,128)(2,1)} %q_ref.3) | copy-start | bytes 1572868
  43.8 28.9 %copy-start.4 = (bf16[256,1024]{1,0:T(8,128)(2,1)S(1)}, bf16[256,1024]{1,0:T(8,128)(2,1)}, u32[]{:S(2)}) copy-start(bf16[256,1024]{1,0:T(8,128)(2,1)} %refs_6_.1) | copy-start | bytes 1572868
  59.7 34.1 %collective-permute-start.15 = (bf16[256,1024]{1,0:T(8,128)(2,1)S(1)}, bf16[256,1024]{1,0:T(8,128)(2,1)S(1)}, u32[]{:S(2)}, u32[]{:S(2)}) collective-permute-start(bf16[256,1024]{1,0:T(8,128)(2,1)S(1)} %get-tuple-element.33), channel_id=1, source_target_pairs={{0,1},{1,0},{2,3},{3,2},{4,5},{5,4},{6,7},{7,6},{8,9},{9,8},{10,11... | collective-permute-start | bytes 1572872 | tf_op jit(solution)/shard_map/ppermute | solution.py:163
  61.1 35.3 %collective-permute-start.16 = (bf16[256,1024]{1,0:T(8,128)(2,1)S(1)}, bf16[256,1024]{1,0:T(8,128)(2,1)S(1)}, u32[]{:S(2)}, u32[]{:S(2)}) collective-permute-start(bf16[256,1024]{1,0:T(8,128)(2,1)S(1)} %get-tuple-element.34), channel_id=1, source_target_pairs={{0,254},{2,0},{4,2},{6,4},{8,6},{10,8},{12,10},{14,12},{16,14},{18... | collective-permute-start | bytes 1572872 | tf_op jit(solution)/shard_map/ppermute | solution.py:168
  61.1 35.3 %collective-permute-start.17 = (bf16[256,1024]{1,0:T(8,128)(2,1)S(1)}, bf16[256,1024]{1,0:T(8,128)(2,1)S(1)}, u32[]{:S(2)}, u32[]{:S(2)}) collective-permute-start(bf16[256,1024]{1,0:T(8,128)(2,1)S(1)} %get-tuple-element.35), channel_id=1, source_target_pairs={{0,2},{2,4},{4,6},{6,8},{8,10},{10,12},{12,14},{14,16},{16,18},{18... | collective-permute-start | bytes 1572872 | tf_op jit(solution)/shard_map/ppermute | solution.py:168
  68.6 32.6 %collective-permute-start.18 = (bf16[256,1024]{1,0:T(8,128)(2,1)S(1)}, bf16[256,1024]{1,0:T(8,128)(2,1)S(1)}, u32[]{:S(2)}, u32[]{:S(2)}) collective-permute-start(bf16[256,1024]{1,0:T(8,128)(2,1)S(1)} %get-tuple-element.36), channel_id=1, source_target_pairs={{0,192},{2,194},{4,196},{6,198},{8,200},{10,202},{12,204},{14,206}... | collective-permute-start | bytes 1572872 | tf_op jit(solution)/shard_map/ppermute | solution.py:168
  71.2 32.9 %collective-permute-start.19 = (bf16[256,1024]{1,0:T(8,128)(2,1)S(1)}, bf16[256,1024]{1,0:T(8,128)(2,1)S(1)}, u32[]{:S(2)}, u32[]{:S(2)}) collective-permute-start(bf16[256,1024]{1,0:T(8,128)(2,1)S(1)} %get-tuple-element.37), channel_id=1, source_target_pairs={{0,64},{2,66},{4,68},{6,70},{8,72},{10,74},{12,76},{14,78},{16,80}... | collective-permute-start | bytes 1572872 | tf_op jit(solution)/shard_map/ppermute | solution.py:168
  93.8 13.3 %collective-permute-start.10 = (bf16[256,1024]{1,0:T(8,128)(2,1)S(1)}, bf16[256,1024]{1,0:T(8,128)(2,1)S(1)}, u32[]{:S(2)}, u32[]{:S(2)}) collective-permute-start(bf16[256,1024]{1,0:T(8,128)(2,1)S(1)} %get-tuple-element.27), channel_id=1, source_target_pairs={{0,1},{1,0},{2,3},{3,2},{4,5},{5,4},{6,7},{7,6},{8,9},{9,8},{10,11... | collective-permute-start | bytes 1572872 | tf_op jit(solution)/shard_map/ppermute | solution.py:163
  96.4 20.3 %collective-permute-start.11 = (bf16[256,1024]{1,0:T(8,128)(2,1)S(1)}, bf16[256,1024]{1,0:T(8,128)(2,1)S(1)}, u32[]{:S(2)}, u32[]{:S(2)}) collective-permute-start(bf16[256,1024]{1,0:T(8,128)(2,1)S(1)} %get-tuple-element.28), channel_id=1, source_target_pairs={{0,254},{2,0},{4,2},{6,4},{8,6},{10,8},{12,10},{14,12},{16,14},{18... | collective-permute-start | bytes 1572872 | tf_op jit(solution)/shard_map/ppermute | solution.py:168
  96.4 26.6 %collective-permute-start.12 = (bf16[256,1024]{1,0:T(8,128)(2,1)S(1)}, bf16[256,1024]{1,0:T(8,128)(2,1)S(1)}, u32[]{:S(2)}, u32[]{:S(2)}) collective-permute-start(bf16[256,1024]{1,0:T(8,128)(2,1)S(1)} %get-tuple-element.29), channel_id=1, source_target_pairs={{0,2},{2,4},{4,6},{6,8},{8,10},{10,12},{12,14},{14,16},{16,18},{18... | collective-permute-start | bytes 1572872 | tf_op jit(solution)/shard_map/ppermute | solution.py:168
  101.1 23.1 %collective-permute-start.13 = (bf16[256,1024]{1,0:T(8,128)(2,1)S(1)}, bf16[256,1024]{1,0:T(8,128)(2,1)S(1)}, u32[]{:S(2)}, u32[]{:S(2)}) collective-permute-start(bf16[256,1024]{1,0:T(8,128)(2,1)S(1)} %get-tuple-element.30), channel_id=1, source_target_pairs={{0,192},{2,194},{4,196},{6,198},{8,200},{10,202},{12,204},{14,206}... | collective-permute-start | bytes 1572872 | tf_op jit(solution)/shard_map/ppermute | solution.py:168
  104.2 27.7 %collective-permute-start.14 = (bf16[256,1024]{1,0:T(8,128)(2,1)S(1)}, bf16[256,1024]{1,0:T(8,128)(2,1)S(1)}, u32[]{:S(2)}, u32[]{:S(2)}) collective-permute-start(bf16[256,1024]{1,0:T(8,128)(2,1)S(1)} %get-tuple-element.31), channel_id=1, source_target_pairs={{0,64},{2,66},{4,68},{6,70},{8,72},{10,74},{12,76},{14,78},{16,80}... | collective-permute-start | bytes 1572872 | tf_op jit(solution)/shard_map/ppermute | solution.py:168

commit v2 on v1

v2 whole, which is shorter than its diff:
```python
import jax
import jax.numpy as jnp
from jax import lax
from jax.experimental import pallas as pl
from jax.experimental.pallas import tpu as pltpu
from jax.sharding import PartitionSpec as P

HD = 64
BT = 128
NSRC = 6
SOURCES = ['own', 'half', 'below', 'pair', 'chip', 'above']
OWN = SOURCES.index("own")
QB = 2
ROWS = QB * BT
PAIR = 2 * HD
F = 1024
PAIRS = F // PAIR
SCALE = HD**-0.5

bf16 = jnp.bfloat16
f32 = jnp.float32


def nt(a, b):
    return lax.dot_general(a, b, (((1,), (1,)), ((), ())), preferred_element_type=f32)


def nn(a, b):
    return lax.dot_general(a, b, (((1,), (0,)), ((), ())), preferred_element_type=f32)


def pick(x, head):
    lanes = lax.broadcasted_iota(jnp.int32, x.shape, 1)
    mine = (lanes < HD) if head == 0 else (lanes >= HD)
    return jnp.where(mine, x, jnp.zeros_like(x))


def merge(x0, x1):
    lanes = lax.broadcasted_iota(jnp.int32, (ROWS, PAIR), 1)
    return jnp.where(lanes < HD, x0, x1)


def pair_cols():
    return pl.ds(pl.multiple_of(pl.program_id(0) * PAIR, PAIR), PAIR)


def source_cols(r):
    return slice(r * ROWS, (r + 1) * ROWS)


def with_own(others, own):
    return [*others[:OWN], own, *others[OWN:]]


def probs_kernel(pattern, own_ref, *refs):
    q_ref, grad_ref = own_ref.at[0], own_ref.at[1]
    k_refs = with_own(refs[: NSRC - 1], own_ref.at[2])
    refs = refs[NSRC - 1 :]
    p_ref, scaled_ref, inv_ref = refs[:3]
    dv_refs = refs[3 : NSRC + 3]
    s_ref = refs[NSRC + 3]
    col = pair_cols()
    at = 2 * pl.program_id(0)
    q = q_ref[:, col]
    invs = []
    for head in range(2):
        qh = pick(q, head)
        for r in range(NSRC):
            s = nt(qh, k_refs[r][:, col])
            for g in range(QB):
                rows = slice(g * BT, (g + 1) * BT)
                for kb in range(QB):
                    part = s[rows, kb * BT : (kb + 1) * BT]
                    if r != OWN or g != kb:
                        part = part + jnp.where(pattern[g, r, kb] == 1, 0.0, -jnp.inf)
                    first = r * ROWS + kb * BT
                    s_ref[head, rows, first : first + BT] = part
        s = s_ref[head]
        peak = jnp.max(s, axis=1, keepdims=True)
        expo = jnp.exp(s - peak)
        invs.append(1.0 / jnp.sum(expo, axis=1, keepdims=True))
        p_ref[at + head] = expo.astype(bf16)
    inv = merge(invs[0], invs[1])
    inv_ref[:, col] = inv
    scaled = (grad_ref[:, col].astype(f32) * inv).astype(bf16)
    scaled_ref[:, col] = scaled
    left0, left1 = pick(scaled, 0).T, pick(scaled, 1).T
    for r in range(NSRC):
        cols = source_cols(r)
        t = nn(left0, p_ref[at, :, cols]) + nn(left1, p_ref[at + 1, :, cols])
        dv_refs[r][:, col] = t.T.astype(bf16)


def grads_kernel(own_ref, scaled_ref, inv_ref, p_ref, *refs):
    q_ref, grad_ref = own_ref.at[0], own_ref.at[1]
    k_refs = with_own(refs[: NSRC - 1], own_ref.at[2])
    v_refs = with_own(refs[NSRC - 1 : 2 * NSRC - 2], own_ref.at[3])
    refs = refs[2 * NSRC - 2 :]
    o_ref, dq_ref = refs[:2]
    dk_refs = refs[2 : NSRC + 2]
    ds_ref = refs[NSRC + 2]
    col = pair_cols()
    at = 2 * pl.program_id(0)

    def rows_of(weights, rights):
        sums = [None, None]
        for head in range(2):
            for r in range(NSRC):
                t = nn(weights(head, source_cols(r)), rights[r][:, col])
                sums[head] = t if r == 0 else sums[head] + t
        return merge(sums[0], sums[1])

    inv = inv_ref[:, col]
    low = (rows_of(lambda head, cols: p_ref[at + head, :, cols], v_refs) * inv).astype(bf16)
    o_ref[:, col] = low
    prod = grad_ref[:, col].astype(f32) * low.astype(f32) * inv
    scaled = scaled_ref[:, col]
    for head in range(2):
        delta = jnp.sum(pick(prod, head), axis=1, keepdims=True)
        left = pick(scaled, head)
        for r in range(NSRC):
            cols = source_cols(r)
            dp = nt(left, v_refs[r][:, col])
            p = p_ref[at + head, :, cols].astype(f32)
            ds_ref[head, :, cols] = (p * (dp - delta)).astype(bf16)
    dq = rows_of(lambda head, cols: ds_ref[head, :, cols], k_refs)
    dq_ref[:, col] = (dq * SCALE).astype(bf16)
    q = q_ref[:, col]
    left0, left1 = pick(q, 0).T, pick(q, 1).T
    for r in range(NSRC):
        cols = source_cols(r)
        t = nn(left0, ds_ref[0, :, cols]) + nn(left1, ds_ref[1, :, cols])
        dk_refs[r][:, col] = t.T.astype(bf16)


whole = pl.BlockSpec(memory_space=pltpu.VMEM)
tall = pltpu.VMEM((ROWS, F), bf16)
PAIR_FLOPS = 2 * 2 * ROWS * NSRC * ROWS * HD


def probs_pass(pattern, own, keys):
    outs = pl.pallas_call(
        probs_kernel,
        grid=(PAIRS,),
        in_specs=[pl.BlockSpec(memory_space=pltpu.SMEM)] + [whole] * NSRC,
        out_specs=[whole] * (3 + NSRC),
        out_shape=[
            pltpu.VMEM((2 * PAIRS, ROWS, NSRC * ROWS), bf16),
            tall,
            pltpu.VMEM((ROWS, F), f32),
        ]
        + [tall] * NSRC,
        scratch_shapes=[pltpu.VMEM((2, ROWS, NSRC * ROWS), f32)],
        compiler_params=pltpu.CompilerParams(vmem_limit_bytes=14 * 2**20),
        cost_estimate=pl.CostEstimate(
            flops=16 * PAIRS * PAIR_FLOPS, bytes_accessed=24 * 2**20, transcendentals=0
        ),
        name="probs_pass",
    )(pattern, own, *keys)
    return outs[0], outs[1], outs[2], outs[3:]


def grads_pass(own, scaled, inv, probs, keys, values):
    outs = pl.pallas_call(
        grads_kernel,
        grid=(PAIRS,),
        in_specs=[whole] * (2 + 2 * NSRC),
        out_specs=[whole] * (2 + NSRC),
        out_shape=[tall] * (2 + NSRC),
        scratch_shapes=[pltpu.VMEM((2, ROWS, NSRC * ROWS), bf16)],
        compiler_params=pltpu.CompilerParams(vmem_limit_bytes=14 * 2**20),
        cost_estimate=pl.CostEstimate(
            flops=24 * PAIRS * PAIR_FLOPS, bytes_accessed=24 * 2**20, transcendentals=0
        ),
        name="grads_pass",
    )(own, scaled, inv, probs, *keys, *values)
    return outs[0], outs[1], outs[2:]


def after(x, *done):
    return lax.optimization_barrier((x, *done))[0] if done else x


def move(x, way, sign):
    if way == "half":
        return lax.ppermute(x, "gz", [(0, 1), (1, 0)])
    peers = lax.axis_size("gx")
    if way in ("below", "above"):
        reach = (peers // 4) * (sign if way == "below" else -sign)
        return lax.ppermute(x, "gx", [(i, (i + reach) % peers) for i in range(peers)])
    first = 0 if way == "chip" else 1
    pairs = [(i, (i + 1) % peers) for i in range(first, peers, 2)]
    return lax.ppermute(x, "gx", pairs + [(b, a) for a, b in pairs])


def local(queries, key_rows, value_rows, grad_out, pattern):
    odd = lax.axis_index("gx") % 2
    at = dict(below=4, above=5, pair=2 + odd, half=1, chip=3 - odd, own=0)
    pattern = jnp.stack(
        [lax.dynamic_index_in_dim(pattern, at[n], 1, keepdims=False) for n in SOURCES], axis=1
    )
    k = {}
    for n in ['below', 'chip', 'pair', 'half', 'above']:
        k[n] = move(key_rows, n, 1)
    v = {}
    for n, deps in [['pair', []], ['half', ['half', 'pair', 'chip']], ['below', ['chip', 'pair']], ['chip', []], ['above', ['chip', 'pair']]]:
        v[n] = move(after(value_rows, *[k[d] for d in deps]), n, 1)
    keys = [k[n] for n in SOURCES if n != "own"]
    values = [v[n] for n in SOURCES if n != "own"]
    own = jnp.stack([queries * bf16(SCALE), grad_out, key_rows, value_rows])
    probs, scaled, inv, terms = probs_pass(pattern, own, keys)
    terms = dict(zip(SOURCES, terms))
    back = dict(own=terms["own"])
    for n, deps in [['below', ['pair', 'half', 'chip']], ['above', []], ['chip', []], ['pair', ['below']], ['half', []]]:
        back[n] = move(after(terms[n], *[v[d] for d in deps]), n, -1)
    total = back["own"].astype(f32)
    for n in ['half', 'chip', 'below', 'pair', 'above']:
        total = total + back[n].astype(f32)
    grad_value = total.astype(bf16)
    attended, grad_query, terms = grads_pass(own, scaled, inv, probs, keys, values)
    terms = dict(zip(SOURCES, terms))
    back2 = dict(own=terms["own"])
    for n, deps in [['below', ['half']], ['half', []], ['pair', ['below']], ['chip', ['below', 'above']], ['above', []]]:
        back2[n] = move(after(terms[n], *[back[d] for d in deps]), n, -1)
    total = back2["own"].astype(f32)
    for n in ['chip', 'above', 'below', 'pair', 'half']:
        total = total + back2[n].astype(f32)
    grad_key = total.astype(bf16)
    return attended, grad_query, grad_key, grad_value


def solution(mesh):
    rows = P(("gx", "gz"), None)
    return jax.shard_map(
        local,
        mesh=mesh,
        in_specs=(rows, rows, rows, rows, P(("gx", "gz"), None, None)),
        out_specs=(rows,) * 4,
        check_vma=False,
    )
```

time: 134 us -> 128 us (0.955)
  Pallas kernels: 37.1 us -> 28.6 us
  waiting for transfers between devices: 46.4 us -> 41.1 us
  starting transfers between devices: 42.4 us -> 47.3 us
  other arithmetic: 2.8 us -> 5.57 us
    pallas_call x1, Pallas kernels: 21.1 us -> 15.2 us  [grads_pass(): pl.pallas_call(grads_kernel, grid=(PAIRS,), in_specs=[whole] * (2 + 2 * N...]
    ppermute x20, waiting for transfers between devices: 46.4 us -> 41.1 us  [the longest x8 19.1 us: move(): lax.ppermute(x, 'gx', [(i, (i + reach) % peers) for i in range(peers)])]
    ppermute x20, starting transfers between devices: 42.4 us -> 47.3 us  [the longest x8 36.9 us: move(): lax.ppermute(x, 'gx', [(i, (i + reach) % peers) for i in range(peers)])]
    another operation x0 -> x2, other arithmetic: none -> 2.77 us  [local(): own = jnp.stack([queries * bf16(SCALE), grad_out, key_rows, value_rows])]
    pallas_call x1, Pallas kernels: 15.9 us -> 13.4 us  [probs_pass(): pl.pallas_call(probs_kernel, grid=(PAIRS,), in_specs=[pl.BlockSpec(memory...]
    unnamed x11 -> x4, local copies, waits for them, and re-layouts: 3.9 us -> 1.59 us
  transfers between devices with their start and end apart: 20 -> 20, of which waited for: 7 -> 7; matrix products, arithmetic and copies ran while one was open for 2% -> 6% of each run, Pallas kernels for 28% -> 23%
where the time goes in v2:
time: 128 us; the launch traced here: 127 us
  starting transfers between devices  47.3 us (37%)
  waiting for transfers between devices  41.1 us (32%)
  Pallas kernels  28.6 us (22%)
  other arithmetic  5.57 us (4%)
  local copies, waits for them, and re-layouts  3.38 us (3%)
    ppermute x8, starting transfers between devices, move(): lax.ppermute(x, 'gx', [(i, (i + reach) % peers) for i in range(peers)])  36.9 us
    ppermute x8, waiting for transfers between devices, move(): lax.ppermute(x, 'gx', [(i, (i + reach) % peers) for i in range(peers)])  19.1 us
    ppermute x8, waiting for transfers between devices, move(): return lax.ppermute(x, 'gx', pairs + [(b, a) for a, b in pairs])  17.9 us
    pallas_call x1, Pallas kernels, grads_pass(): pl.pallas_call(grads_kernel, grid=(PAIRS,), in_specs=[whole] * (2 + 2 * N...  15.2 us
    pallas_call x1, Pallas kernels, probs_pass(): pl.pallas_call(probs_kernel, grid=(PAIRS,), in_specs=[pl.BlockSpec(memory...  13.4 us
    ppermute x8, starting transfers between devices, move(): return lax.ppermute(x, 'gx', pairs + [(b, a) for a, b in pairs])  6.82 us
    ppermute x4, waiting for transfers between devices, move(): return lax.ppermute(x, 'gz', [(0, 1), (1, 0)])  4.16 us
    ppermute x4, starting transfers between devices, move(): return lax.ppermute(x, 'gz', [(0, 1), (1, 0)])  3.54 us
  transfers between devices with their start and end apart: 20, of which 7 were waited for; matrix products, arithmetic and copies ran while one was open for 6% of the time, Pallas kernels for 23%

profile of v2, /device:TPU:59, one launch (start us, length us, event | category | flops | bytes accessed | tf_op | source)
XLA Modules:
  0.0 126.7 jit_solution(5204427710316395425)
XLA Ops:
  0.6 1.9 %collective-permute-start.2 = (bf16[256,1024]{1,0:T(8,128)(2,1)}, bf16[256,1024]{1,0:T(8,128)(2,1)S(1)}, u32[]{:S(2)}, u32[]{:S(2)}) collective-permute-start(bf16[256,1024]{1,0:T(8,128)(2,1)} %param.6), channel_id=1, source_target_pairs={{2,4},{6,8},{10,12},{14,16},{18,20},{22,24},{26,28},{30,32},{34,36... | collective-permute-start | bytes 1572872 | tf_op jit(solution)/shard_map/ppermute | solution.py:193
  2.5 0.0 collective-permute-start.3
  2.5 2.1 %collective-permute-start = (bf16[256,1024]{1,0:T(8,128)(2,1)}, bf16[256,1024]{1,0:T(8,128)(2,1)S(1)}, u32[]{:S(2)}, u32[]{:S(2)}) collective-permute-start(bf16[256,1024]{1,0:T(8,128)(2,1)} %param.6), channel_id=1, source_target_pairs={{0,1},{1,0},{2,3},{3,2},{4,5},{5,4},{6,7},{7,6},{8,9},{9,8},{10,11... | collective-permute-start | bytes 1572872 | tf_op jit(solution)/shard_map/ppermute | solution.py:186
  4.7 4.2 %collective-permute-start.1 = (bf16[256,1024]{1,0:T(8,128)(2,1)}, bf16[256,1024]{1,0:T(8,128)(2,1)S(1)}, u32[]{:S(2)}, u32[]{:S(2)}) collective-permute-start(bf16[256,1024]{1,0:T(8,128)(2,1)} %param.6), channel_id=1, source_target_pairs={{0,64},{2,66},{4,68},{6,70},{8,72},{10,74},{12,76},{14,78},{16,80}... | collective-permute-start | bytes 1572872 | tf_op jit(solution)/shard_map/ppermute | solution.py:190
  8.9 0.0 collective-permute-start.4
  8.9 0.9 fusion
  9.8 0.8 stack.29
  10.6 0.1 copy.14.pattern
  10.7 1.1 multiply_bitcast_fusion
  11.8 0.0 copy-start
  11.8 1.7 %pad_maximum_fusion.own_ref = bf16[4,256,1024]{2,1,0:T(8,128)(2,1)S(1)} fusion(bf16[1,256,1024]{2,1,0:T(8,128)(2,1)} %bitcast.8, bf16[1,256,1024]{2,1,0:T(8,128)(2,1)} %bitcast.7, bf16[1,256,1024]{2,1,0:T(8,128)(2,1)} %bitcast.6, bf16[1,256,1024]{2,1,0:T(8,128)(2,1)S(1)} %multiply_bitcast_fusion), kind=kLoop, calls=%fused_computation | loop fusion | flops 3145728 | bytes 4194304 | tf_op jit(solution)/shard_map/stack | solution.py:210
  13.5 0.0 collective-permute-done.2.refs_2_
  13.5 0.0 copy-done
  13.5 4.8 %collective-permute-start.7 = (bf16[256,1024]{1,0:T(8,128)(2,1)S(1)}, bf16[256,1024]{1,0:T(8,128)(2,1)S(1)}, u32[]{:S(2)}, u32[]{:S(2)}) collective-permute-start(bf16[256,1024]{1,0:T(8,128)(2,1)S(1)} %copy-done), channel_id=1, source_target_pairs={{2,4},{6,8},{10,12},{14,16},{18,20},{22,24},{26,28},{30,32},{34,36... | collective-permute-start | bytes 1572872 | tf_op jit(solution)/shard_map/ppermute | solution.py:193
  18.3 0.0 collective-permute-done.3.refs_3_
  18.3 0.0 collective-permute-start.8
  18.3 4.1 %collective-permute-done.refs_0_ = bf16[256,1024]{1,0:T(8,128)(2,1)S(1)} collective-permute-done((bf16[256,1024]{1,0:T(8,128)(2,1)}, bf16[256,1024]{1,0:T(8,128)(2,1)S(1)}, u32[]{:S(2)}, u32[]{:S(2)}) %collective-permute-start) | collective-permute-done | bytes 524320 | tf_op jit(solution)/shard_map/ppermute | solution.py:186
  22.4 9.2 %collective-permute-start.6 = (bf16[256,1024]{1,0:T(8,128)(2,1)S(1)}, bf16[256,1024]{1,0:T(8,128)(2,1)S(1)}, u32[]{:S(2)}, u32[]{:S(2)}) collective-permute-start(bf16[256,1024]{1,0:T(8,128)(2,1)S(1)} %copy-done), channel_id=1, source_target_pairs={{0,64},{2,66},{4,68},{6,70},{8,72},{10,74},{12,76},{14,78},{16,80}... | collective-permute-start | bytes 1572872 | tf_op jit(solution)/shard_map/ppermute | solution.py:190
  31.7 5.7 %collective-permute-done.1.refs_1_ = bf16[256,1024]{1,0:T(8,128)(2,1)S(1)} collective-permute-done((bf16[256,1024]{1,0:T(8,128)(2,1)}, bf16[256,1024]{1,0:T(8,128)(2,1)S(1)}, u32[]{:S(2)}, u32[]{:S(2)}) %collective-permute-start.1) | collective-permute-done | bytes 524320 | tf_op jit(solution)/shard_map/ppermute | solution.py:190
  37.4 2.5 %collective-permute-start.9 = (bf16[256,1024]{1,0:T(8,128)(2,1)S(1)}, bf16[256,1024]{1,0:T(8,128)(2,1)S(1)}, u32[]{:S(2)}, u32[]{:S(2)}) collective-permute-start(bf16[256,1024]{1,0:T(8,128)(2,1)S(1)} %copy-done), channel_id=1, source_target_pairs={{0,192},{2,194},{4,196},{6,198},{8,200},{10,202},{12,204},{14,206}... | collective-permute-start | bytes 1572872 | tf_op jit(solution)/shard_map/ppermute | solution.py:190
  39.9 0.0 collective-permute-done.4.refs_4_
  39.9 0.2 collective-permute-start.5
  40.1 13.4 %probs_pass.1 = (bf16[16,256,1536]{2,1,0:T(8,128)(2,1)S(1)}, bf16[256,1024]{1,0:T(8,128)(2,1)S(1)}, f32[256,1024]{1,0:T(8,128)S(1)}, bf16[256,1024]{1,0:T(8,128)...) custom-call(s32[2,6,2]{2,1,0:T(8,128)S(1)} %copy.14.pattern, ...), custom_call_target="tpu_custom_call" | custom-call | flops 12884901888 | bytes 25165824 | tf_op jit(solution)/shard_map/probs_pass/pallas_call | solution.py:142
  53.6 0.0 collective-permute-done.7.refs_7_
  53.6 15.3 %collective-permute-start.11 = (bf16[256,1024]{1,0:T(8,128)(2,1)S(1)}, bf16[256,1024]{1,0:T(8,128)(2,1)S(1)}, u32[]{:S(2)}, u32[]{:S(2)}) collective-permute-start(bf16[256,1024]{1,0:T(8,128)(2,1)S(1)} %get-tuple-element.39), channel_id=1, source_target_pairs={{0,64},{2,66},{4,68},{6,70},{8,72},{10,74},{12,76},{14,78},{16,80}... | collective-permute-start | bytes 1572872 | tf_op jit(solution)/shard_map/ppermute | solution.py:190
  68.9 0.0 collective-permute-done.8.refs_8_
  68.9 0.0 collective-permute-start.14
  68.9 0.0 collective-permute-done.5.refs_5_
  68.9 0.1 collective-permute-start.18
  69.0 9.8 %collective-permute-done.6.refs_6_ = bf16[256,1024]{1,0:T(8,128)(2,1)S(1)} collective-permute-done((bf16[256,1024]{1,0:T(8,128)(2,1)S(1)}, bf16[256,1024]{1,0:T(8,128)(2,1)S(1)}, u32[]{:S(2)}, u32[]{:S(2)}) %collective-permute-start.6) | collective-permute-done | bytes 524320 | tf_op jit(solution)/shard_map/ppermute | solution.py:190
  78.8 3.2 %collective-permute-start.10 = (bf16[256,1024]{1,0:T(8,128)(2,1)S(1)}, bf16[256,1024]{1,0:T(8,128)(2,1)S(1)}, u32[]{:S(2)}, u32[]{:S(2)}) collective-permute-start(bf16[256,1024]{1,0:T(8,128)(2,1)S(1)} %get-tuple-element.38), channel_id=1, source_target_pairs={{0,192},{2,194},{4,196},{6,198},{8,200},{10,202},{12,204},{14,206}... | collective-permute-start | bytes 1572872 | tf_op jit(solution)/shard_map/ppermute | solution.py:190
  82.1 0.0 collective-permute-done.9.refs_9_
  82.1 0.0 collective-permute-start.19
  82.1 15.2 %grads_pass.1 = (bf16[256,1024]{1,0:T(8,128)(2,1)S(1)}, bf16[256,1024]{1,0:T(8,128)(2,1)S(1)}, bf16[256,1024]{1,0:T(8,128)(2,1)S(1)}, bf16[256,1024]{1,0:T(8,128...) custom-call(bf16[4,256,1024]{2,1,0:T(8,128)(2,1)S(1)} %pad_maximum_f, ...), custom_call_target="tpu_custom_call" | custom-call | flops 19327352832 | bytes 25165824 | tf_op jit(solution)/shard_map/grads_pass/pallas_call | solution.py:164
  97.2 0.0 collective-permute-done.14
  97.3 2.3 %collective-permute-start.15 = (bf16[256,1024]{1,0:T(8,128)(2,1)S(1)}, bf16[256,1024]{1,0:T(8,128)(2,1)S(1)}, u32[]{:S(2)}, u32[]{:S(2)}) collective-permute-start(bf16[256,1024]{1,0:T(8,128)(2,1)S(1)} %get-tuple-element.44), channel_id=1, source_target_pairs={{0,192},{2,194},{4,196},{6,198},{8,200},{10,202},{12,204},{14,206}... | collective-permute-start | bytes 1572872 | tf_op jit(solution)/shard_map/ppermute | solution.py:190
  99.6 0.0 collective-permute-done.11
  99.6 0.1 collective-permute-start.13
  99.7 3.4 %collective-permute-done.10 = bf16[256,1024]{1,0:T(8,128)(2,1)S(1)} collective-permute-done((bf16[256,1024]{1,0:T(8,128)(2,1)S(1)}, bf16[256,1024]{1,0:T(8,128)(2,1)S(1)}, u32[]{:S(2)}, u32[]{:S(2)}) %collective-permute-start.10) | collective-permute-done | bytes 524320 | tf_op jit(solution)/shard_map/ppermute | solution.py:190
  103.1 1.2 collective-permute-start.17
  104.3 0.0 collective-permute-done.18
  104.3 0.0 collective-permute-start.12
  104.3 6.5 %collective-permute-done.19 = bf16[256,1024]{1,0:T(8,128)(2,1)S(1)} collective-permute-done((bf16[256,1024]{1,0:T(8,128)(2,1)S(1)}, bf16[256,1024]{1,0:T(8,128)(2,1)S(1)}, u32[]{:S(2)}, u32[]{:S(2)}) %collective-permute-start.19) | collective-permute-done | bytes 524320 | tf_op jit(solution)/shard_map/ppermute | solution.py:193
  110.7 0.0 collective-permute-start.16
  110.7 0.8 copy.15
  111.5 0.8 copy.16
  112.3 1.4 %add_convert_fusion = bf16[256,1024]{1,0:T(8,128)(2,1)} fusion(bf16[256,1024]{1,0:T(8,128)(2,1)S(1)} %collective-permute-done.11, bf16[256,1024]{1,0:T(8,128)(2,1)S(1)} %collective-permute-done.19, bf16[256,1024]{1,0:T(8,128)(2,1)S(1)} %collective-permute-done.10, bf16[256,1024]{1,0:T(8,128)(2,1)S(1)} %collective-permute-done.18, ...), kind=kLoop, calls=%fused_computation.1 | loop fusion | flops 3145728 | bytes 3670016 | tf_op jit(solution)/shard_map/convert_element_type | solution.py:219
  113.7 0.0 collective-permute-done.15
  113.7 0.1 collective-permute-done.13
  113.9 0.0 collective-permute-done.17
  113.9 0.0 collective-permute-done.12
  113.9 11.4 %collective-permute-done.16 = bf16[256,1024]{1,0:T(8,128)(2,1)S(1)} collective-permute-done((bf16[256,1024]{1,0:T(8,128)(2,1)S(1)}, bf16[256,1024]{1,0:T(8,128)(2,1)S(1)}, u32[]{:S(2)}, u32[]{:S(2)}) %collective-permute-start.16) | collective-permute-done | bytes 524320 | tf_op jit(solution)/shard_map/ppermute | solution.py:193
  125.3 1.4 %add_convert_fusion.1 = bf16[256,1024]{1,0:T(8,128)(2,1)} fusion(bf16[256,1024]{1,0:T(8,128)(2,1)S(1)} %collective-permute-done.17, bf16[256,1024]{1,0:T(8,128)(2,1)S(1)} %collective-permute-done.16, bf16[256,1024]{1,0:T(8,128)(2,1)S(1)} %collective-permute-done.15, bf16[256,1024]{1,0:T(8,128)(2,1)S(1)} %collective-permute-done.13, ...), kind=kLoop, calls=%fused_computation.2 | loop fusion | flops 3145728 | bytes 3670016 | tf_op jit(solution)/shard_map/convert_element_type | solution.py:228
Async XLA Ops:
  0.6 12.8 %collective-permute-start.2 = (bf16[256,1024]{1,0:T(8,128)(2,1)}, bf16[256,1024]{1,0:T(8,128)(2,1)S(1)}, u32[]{:S(2)}, u32[]{:S(2)}) collective-permute-start(bf16[256,1024]{1,0:T(8,128)(2,1)} %param.6), channel_id=1, source_target_pairs={{2,4},{6,8},{10,12},{14,16},{18,20},{22,24},{26,28},{30,32},{34,36... | collective-permute-start | bytes 1572872 | tf_op jit(solution)/shard_map/ppermute | solution.py:193
  2.5 15.7 %collective-permute-start.3 = (bf16[256,1024]{1,0:T(8,128)(2,1)}, bf16[256,1024]{1,0:T(8,128)(2,1)S(1)}, u32[]{:S(2)}, u32[]{:S(2)}) collective-permute-start(bf16[256,1024]{1,0:T(8,128)(2,1)} %param.6), channel_id=1, source_target_pairs={{0,2},{4,6},{8,10},{12,14},{16,18},{20,22},{24,26},{28,30},{32,34}... | collective-permute-start | bytes 1572872 | tf_op jit(solution)/shard_map/ppermute | solution.py:193
  2.5 19.9 %collective-permute-start = (bf16[256,1024]{1,0:T(8,128)(2,1)}, bf16[256,1024]{1,0:T(8,128)(2,1)S(1)}, u32[]{:S(2)}, u32[]{:S(2)}) collective-permute-start(bf16[256,1024]{1,0:T(8,128)(2,1)} %param.6), channel_id=1, source_target_pairs={{0,1},{1,0},{2,3},{3,2},{4,5},{5,4},{6,7},{7,6},{8,9},{9,8},{10,11... | collective-permute-start | bytes 1572872 | tf_op jit(solution)/shard_map/ppermute | solution.py:186
  4.7 32.7 %collective-permute-start.1 = (bf16[256,1024]{1,0:T(8,128)(2,1)}, bf16[256,1024]{1,0:T(8,128)(2,1)S(1)}, u32[]{:S(2)}, u32[]{:S(2)}) collective-permute-start(bf16[256,1024]{1,0:T(8,128)(2,1)} %param.6), channel_id=1, source_target_pairs={{0,64},{2,66},{4,68},{6,70},{8,72},{10,74},{12,76},{14,78},{16,80}... | collective-permute-start | bytes 1572872 | tf_op jit(solution)/shard_map/ppermute | solution.py:190
  8.9 31.0 %collective-permute-start.4 = (bf16[256,1024]{1,0:T(8,128)(2,1)}, bf16[256,1024]{1,0:T(8,128)(2,1)S(1)}, u32[]{:S(2)}, u32[]{:S(2)}) collective-permute-start(bf16[256,1024]{1,0:T(8,128)(2,1)} %param.6), channel_id=1, source_target_pairs={{0,192},{2,194},{4,196},{6,198},{8,200},{10,202},{12,204},{14,206}... | collective-permute-start | bytes 1572872 | tf_op jit(solution)/shard_map/ppermute | solution.py:190
  11.8 1.7 %copy-start = (bf16[256,1024]{1,0:T(8,128)(2,1)S(1)}, bf16[256,1024]{1,0:T(8,128)(2,1)}, u32[]{:S(2)}) copy-start(bf16[256,1024]{1,0:T(8,128)(2,1)} %param.7) | copy-start | bytes 1572868
  13.5 40.1 %collective-permute-start.7 = (bf16[256,1024]{1,0:T(8,128)(2,1)S(1)}, bf16[256,1024]{1,0:T(8,128)(2,1)S(1)}, u32[]{:S(2)}, u32[]{:S(2)}) collective-permute-start(bf16[256,1024]{1,0:T(8,128)(2,1)S(1)} %copy-done), channel_id=1, source_target_pairs={{2,4},{6,8},{10,12},{14,16},{18,20},{22,24},{26,28},{30,32},{34,36... | collective-permute-start | bytes 1572872 | tf_op jit(solution)/shard_map/ppermute | solution.py:193
  18.3 50.6 %collective-permute-start.8 = (bf16[256,1024]{1,0:T(8,128)(2,1)S(1)}, bf16[256,1024]{1,0:T(8,128)(2,1)S(1)}, u32[]{:S(2)}, u32[]{:S(2)}) collective-permute-start(bf16[256,1024]{1,0:T(8,128)(2,1)S(1)} %copy-done), channel_id=1, source_target_pairs={{0,2},{4,6},{8,10},{12,14},{16,18},{20,22},{24,26},{28,30},{32,34}... | collective-permute-start | bytes 1572872 | tf_op jit(solution)/shard_map/ppermute | solution.py:193
  22.4 56.4 %collective-permute-start.6 = (bf16[256,1024]{1,0:T(8,128)(2,1)S(1)}, bf16[256,1024]{1,0:T(8,128)(2,1)S(1)}, u32[]{:S(2)}, u32[]{:S(2)}) collective-permute-start(bf16[256,1024]{1,0:T(8,128)(2,1)S(1)} %copy-done), channel_id=1, source_target_pairs={{0,64},{2,66},{4,68},{6,70},{8,72},{10,74},{12,76},{14,78},{16,80}... | collective-permute-start | bytes 1572872 | tf_op jit(solution)/shard_map/ppermute | solution.py:190
  37.4 44.7 %collective-permute-start.9 = (bf16[256,1024]{1,0:T(8,128)(2,1)S(1)}, bf16[256,1024]{1,0:T(8,128)(2,1)S(1)}, u32[]{:S(2)}, u32[]{:S(2)}) collective-permute-start(bf16[256,1024]{1,0:T(8,128)(2,1)S(1)} %copy-done), channel_id=1, source_target_pairs={{0,192},{2,194},{4,196},{6,198},{8,200},{10,202},{12,204},{14,206}... | collective-permute-start | bytes 1572872 | tf_op jit(solution)/shard_map/ppermute | solution.py:190
  39.9 29.0 %collective-permute-start.5 = (bf16[256,1024]{1,0:T(8,128)(2,1)S(1)}, bf16[256,1024]{1,0:T(8,128)(2,1)S(1)}, u32[]{:S(2)}, u32[]{:S(2)}) collective-permute-start(bf16[256,1024]{1,0:T(8,128)(2,1)S(1)} %copy-done), channel_id=1, source_target_pairs={{0,1},{1,0},{2,3},{3,2},{4,5},{5,4},{6,7},{7,6},{8,9},{9,8},{10,11... | collective-permute-start | bytes 1572872 | tf_op jit(solution)/shard_map/ppermute | solution.py:186
  53.6 46.0 %collective-permute-start.11 = (bf16[256,1024]{1,0:T(8,128)(2,1)S(1)}, bf16[256,1024]{1,0:T(8,128)(2,1)S(1)}, u32[]{:S(2)}, u32[]{:S(2)}) collective-permute-start(bf16[256,1024]{1,0:T(8,128)(2,1)S(1)} %get-tuple-element.39), channel_id=1, source_target_pairs={{0,64},{2,66},{4,68},{6,70},{8,72},{10,74},{12,76},{14,78},{16,80}... | collective-permute-start | bytes 1572872 | tf_op jit(solution)/shard_map/ppermute | solution.py:190
  68.9 28.3 %collective-permute-start.14 = (bf16[256,1024]{1,0:T(8,128)(2,1)S(1)}, bf16[256,1024]{1,0:T(8,128)(2,1)S(1)}, u32[]{:S(2)}, u32[]{:S(2)}) collective-permute-start(bf16[256,1024]{1,0:T(8,128)(2,1)S(1)} %get-tuple-element.43), channel_id=1, source_target_pairs={{0,1},{1,0},{2,3},{3,2},{4,5},{5,4},{6,7},{7,6},{8,9},{9,8},{10,11... | collective-permute-start | bytes 1572872 | tf_op jit(solution)/shard_map/ppermute | solution.py:186
  68.9 35.4 %collective-permute-start.18 = (bf16[256,1024]{1,0:T(8,128)(2,1)S(1)}, bf16[256,1024]{1,0:T(8,128)(2,1)S(1)}, u32[]{:S(2)}, u32[]{:S(2)}) collective-permute-start(bf16[256,1024]{1,0:T(8,128)(2,1)S(1)} %get-tuple-element.49), channel_id=1, source_target_pairs={{0,2},{4,6},{8,10},{12,14},{16,18},{20,22},{24,26},{28,30},{32,34}... | collective-permute-start | bytes 1572872 | tf_op jit(solution)/shard_map/ppermute | solution.py:193
  78.8 24.3 %collective-permute-start.10 = (bf16[256,1024]{1,0:T(8,128)(2,1)S(1)}, bf16[256,1024]{1,0:T(8,128)(2,1)S(1)}, u32[]{:S(2)}, u32[]{:S(2)}) collective-permute-start(bf16[256,1024]{1,0:T(8,128)(2,1)S(1)} %get-tuple-element.38), channel_id=1, source_target_pairs={{0,192},{2,194},{4,196},{6,198},{8,200},{10,202},{12,204},{14,206}... | collective-permute-start | bytes 1572872 | tf_op jit(solution)/shard_map/ppermute | solution.py:190
  82.1 28.7 %collective-permute-start.19 = (bf16[256,1024]{1,0:T(8,128)(2,1)S(1)}, bf16[256,1024]{1,0:T(8,128)(2,1)S(1)}, u32[]{:S(2)}, u32[]{:S(2)}) collective-permute-start(bf16[256,1024]{1,0:T(8,128)(2,1)S(1)} %get-tuple-element.51), channel_id=1, source_target_pairs={{2,4},{6,8},{10,12},{14,16},{18,20},{22,24},{26,28},{30,32},{34,36... | collective-permute-start | bytes 1572872 | tf_op jit(solution)/shard_map/ppermute | solution.py:193
  97.3 16.5 %collective-permute-start.15 = (bf16[256,1024]{1,0:T(8,128)(2,1)S(1)}, bf16[256,1024]{1,0:T(8,128)(2,1)S(1)}, u32[]{:S(2)}, u32[]{:S(2)}) collective-permute-start(bf16[256,1024]{1,0:T(8,128)(2,1)S(1)} %get-tuple-element.44), channel_id=1, source_target_pairs={{0,192},{2,194},{4,196},{6,198},{8,200},{10,202},{12,204},{14,206}... | collective-permute-start | bytes 1572872 | tf_op jit(solution)/shard_map/ppermute | solution.py:190
  99.6 14.3 %collective-permute-start.13 = (bf16[256,1024]{1,0:T(8,128)(2,1)S(1)}, bf16[256,1024]{1,0:T(8,128)(2,1)S(1)}, u32[]{:S(2)}, u32[]{:S(2)}) collective-permute-start(bf16[256,1024]{1,0:T(8,128)(2,1)S(1)} %get-tuple-element.41), channel_id=1, source_target_pairs={{0,64},{2,66},{4,68},{6,70},{8,72},{10,74},{12,76},{14,78},{16,80}... | collective-permute-start | bytes 1572872 | tf_op jit(solution)/shard_map/ppermute | solution.py:190
  103.1 10.8 %collective-permute-start.17 = (bf16[256,1024]{1,0:T(8,128)(2,1)S(1)}, bf16[256,1024]{1,0:T(8,128)(2,1)S(1)}, u32[]{:S(2)}, u32[]{:S(2)}) collective-permute-start(bf16[256,1024]{1,0:T(8,128)(2,1)S(1)} %get-tuple-element.47), channel_id=1, source_target_pairs={{0,1},{1,0},{2,3},{3,2},{4,5},{5,4},{6,7},{7,6},{8,9},{9,8},{10,11... | collective-permute-start | bytes 1572872 | tf_op jit(solution)/shard_map/ppermute | solution.py:186
  104.3 9.6 %collective-permute-start.12 = (bf16[256,1024]{1,0:T(8,128)(2,1)S(1)}, bf16[256,1024]{1,0:T(8,128)(2,1)S(1)}, u32[]{:S(2)}, u32[]{:S(2)}) collective-permute-start(bf16[256,1024]{1,0:T(8,128)(2,1)S(1)} %get-tuple-element.40), channel_id=1, source_target_pairs={{0,2},{4,6},{8,10},{12,14},{16,18},{20,22},{24,26},{28,30},{32,34}... | collective-permute-start | bytes 1572872 | tf_op jit(solution)/shard_map/ppermute | solution.py:193
  110.7 14.5 %collective-permute-start.16 = (bf16[256,1024]{1,0:T(8,128)(2,1)S(1)}, bf16[256,1024]{1,0:T(8,128)(2,1)S(1)}, u32[]{:S(2)}, u32[]{:S(2)}) collective-permute-start(bf16[256,1024]{1,0:T(8,128)(2,1)S(1)} %get-tuple-element.46), channel_id=1, source_target_pairs={{2,4},{6,8},{10,12},{14,16},{18,20},{22,24},{26,28},{30,32},{34,36... | collective-permute-start | bytes 1572872 | tf_op jit(solution)/shard_map/ppermute | solution.py:193

commit v3 on v2

--- a/solution.py
+++ b/solution.py
@@ -8,7 +8,7 @@
 HD = 64
 BT = 128
 NSRC = 6
-SOURCES = ['own', 'half', 'below', 'pair', 'chip', 'above']
+SOURCES = ['above', 'pair', 'own', 'half', 'below', 'chip']
 OWN = SOURCES.index("own")
 QB = 2
 ROWS = QB * BT
@@ -188,9 +188,8 @@
     if way in ("below", "above"):
         reach = (peers // 4) * (sign if way == "below" else -sign)
         return lax.ppermute(x, "gx", [(i, (i + reach) % peers) for i in range(peers)])
-    first = 0 if way == "chip" else 1
-    pairs = [(i, (i + 1) % peers) for i in range(first, peers, 2)]
-    return lax.ppermute(x, "gx", pairs + [(b, a) for a, b in pairs])
+    ends = [(i, (i + 1) % peers) for i in range(0 if way == "chip" else 1, peers, 2)]
+    return lax.ppermute(x, "gx", ends + [(b, a) for a, b in ends])
 
 
 def local(queries, key_rows, value_rows, grad_out, pattern):
@@ -199,20 +198,22 @@
     pattern = jnp.stack(
         [lax.dynamic_index_in_dim(pattern, at[n], 1, keepdims=False) for n in SOURCES], axis=1
     )
+    own = jnp.stack([queries * bf16(SCALE), grad_out, key_rows, value_rows])
     k = {}
-    for n in ['below', 'chip', 'pair', 'half', 'above']:
+    for n in ['chip', 'below', 'half', 'above', 'pair']:
         k[n] = move(key_rows, n, 1)
     v = {}
     for n, deps in [['pair', []], ['half', ['half', 'pair', 'chip']], ['below', ['chip', 'pair']], ['chip', []], ['above', ['chip', 'pair']]]:
-        v[n] = move(after(value_rows, *[k[d] for d in deps]), n, 1)
+        x = after(value_rows, *[k[d] for d in deps])
+        v[n] = move(x, n, 1)
     keys = [k[n] for n in SOURCES if n != "own"]
     values = [v[n] for n in SOURCES if n != "own"]
-    own = jnp.stack([queries * bf16(SCALE), grad_out, key_rows, value_rows])
     probs, scaled, inv, terms = probs_pass(pattern, own, keys)
     terms = dict(zip(SOURCES, terms))
     back = dict(own=terms["own"])
     for n, deps in [['below', ['pair', 'half', 'chip']], ['above', []], ['chip', []], ['pair', ['below']], ['half', []]]:
-        back[n] = move(after(terms[n], *[v[d] for d in deps]), n, -1)
+        x = after(terms[n], *[v[d] for d in deps])
+        back[n] = move(x, n, -1)
     total = back["own"].astype(f32)
     for n in ['half', 'chip', 'below', 'pair', 'above']:
         total = total + back[n].astype(f32)
@@ -223,7 +224,7 @@
     for n, deps in [['below', ['half']], ['half', []], ['pair', ['below']], ['chip', ['below', 'above']], ['above', []]]:
         back2[n] = move(after(terms[n], *[back[d] for d in deps]), n, -1)
     total = back2["own"].astype(f32)
-    for n in ['chip', 'above', 'below', 'pair', 'half']:
+    for n in ['above', 'chip', 'pair', 'half', 'below']:
         total = total + back2[n].astype(f32)
     grad_key = total.astype(bf16)
     return attended, grad_query, grad_key, grad_value

time: 128 us -> 126 us (0.984)
  starting transfers between devices: 47.3 us -> 42.7 us
  waiting for transfers between devices: 41.1 us -> 42.8 us
    ppermute x8, waiting for transfers between devices: 19.1 us -> 30.1 us  [move(): lax.ppermute(x, 'gx', [(i, (i + reach) % peers) for i in range(peers)])]
    ppermute x8, starting transfers between devices: 36.9 us -> 26 us  [move(): lax.ppermute(x, 'gx', [(i, (i + reach) % peers) for i in range(peers)])]
    ppermute x8, waiting for transfers between devices: 17.9 us -> 8.01 us  [move(): return lax.ppermute(x, 'gx', ends + [(b, a) for a, b in ends])]
    ppermute x8, starting transfers between devices: 6.82 us -> 11.6 us  [move(): return lax.ppermute(x, 'gx', ends + [(b, a) for a, b in ends])]
    ppermute x4, starting transfers between devices: 3.54 us -> 5.14 us  [move(): return lax.ppermute(x, 'gz', [(0, 1), (1, 0)])]
  transfers between devices with their start and end apart: 20 -> 20, of which waited for: 7 -> 9; matrix products, arithmetic and copies ran while one was open for 6% -> 6% of each run, Pallas kernels for 23% -> 23%
where the time goes in v3:
time: 126 us; the launch traced here: 124 us
  waiting for transfers between devices  42.8 us (34%)
  starting transfers between devices  42.7 us (34%)
  Pallas kernels  28.5 us (23%)
  other arithmetic  5.57 us (4%)
  local copies, waits for them, and re-layouts  3.37 us (3%)
    ppermute x8, waiting for transfers between devices, move(): lax.ppermute(x, 'gx', [(i, (i + reach) % peers) for i in range(peers)])  30.1 us
    ppermute x8, starting transfers between devices, move(): lax.ppermute(x, 'gx', [(i, (i + reach) % peers) for i in range(peers)])  26 us
    pallas_call x1, Pallas kernels, grads_pass(): pl.pallas_call(grads_kernel, grid=(PAIRS,), in_specs=[whole] * (2 + 2 * N...  15.1 us
    pallas_call x1, Pallas kernels, probs_pass(): pl.pallas_call(probs_kernel, grid=(PAIRS,), in_specs=[pl.BlockSpec(memory...  13.5 us
    ppermute x8, starting transfers between devices, move(): return lax.ppermute(x, 'gx', ends + [(b, a) for a, b in ends])  11.6 us
    ppermute x8, waiting for transfers between devices, move(): return lax.ppermute(x, 'gx', ends + [(b, a) for a, b in ends])  8.01 us
    ppermute x4, starting transfers between devices, move(): return lax.ppermute(x, 'gz', [(0, 1), (1, 0)])  5.14 us
    ppermute x4, waiting for transfers between devices, move(): return lax.ppermute(x, 'gz', [(0, 1), (1, 0)])  4.66 us
  transfers between devices with their start and end apart: 20, of which 9 were waited for; matrix products, arithmetic and copies ran while one was open for 6% of the time, Pallas kernels for 23%

profile of v3, /device:TPU:59, one launch (start us, length us, event | category | flops | bytes accessed | tf_op | source)
XLA Modules:
  0.0 123.7 jit_solution(12291362128694878347)
XLA Ops:
  0.6 1.9 %collective-permute-start.1 = (bf16[256,1024]{1,0:T(8,128)(2,1)}, bf16[256,1024]{1,0:T(8,128)(2,1)S(1)}, u32[]{:S(2)}, u32[]{:S(2)}) collective-permute-start(bf16[256,1024]{1,0:T(8,128)(2,1)} %param.6), channel_id=1, source_target_pairs={{2,4},{6,8},{10,12},{14,16},{18,20},{22,24},{26,28},{30,32},{34,36... | collective-permute-start | bytes 1572872 | tf_op jit(solution)/shard_map/ppermute | solution.py:192
  2.5 0.0 collective-permute-start.4
  2.5 2.1 %collective-permute-start.2 = (bf16[256,1024]{1,0:T(8,128)(2,1)}, bf16[256,1024]{1,0:T(8,128)(2,1)S(1)}, u32[]{:S(2)}, u32[]{:S(2)}) collective-permute-start(bf16[256,1024]{1,0:T(8,128)(2,1)} %param.6), channel_id=1, source_target_pairs={{0,1},{1,0},{2,3},{3,2},{4,5},{5,4},{6,7},{7,6},{8,9},{9,8},{10,11... | collective-permute-start | bytes 1572872 | tf_op jit(solution)/shard_map/ppermute | solution.py:186
  4.7 3.9 %collective-permute-start = (bf16[256,1024]{1,0:T(8,128)(2,1)}, bf16[256,1024]{1,0:T(8,128)(2,1)S(1)}, u32[]{:S(2)}, u32[]{:S(2)}) collective-permute-start(bf16[256,1024]{1,0:T(8,128)(2,1)} %param.6), channel_id=1, source_target_pairs={{0,192},{2,194},{4,196},{6,198},{8,200},{10,202},{12,204},{14,206}... | collective-permute-start | bytes 1572872 | tf_op jit(solution)/shard_map/ppermute | solution.py:190
  8.5 0.4 collective-permute-start.3
  8.9 0.9 constant_dynamic-slice_fusion
  9.8 0.8 stack.29
  10.6 0.1 copy.14.pattern
  10.7 1.1 multiply_bitcast_fusion
  11.8 0.0 copy-start
  11.8 1.7 %pad_maximum_fusion.own_ref = bf16[4,256,1024]{2,1,0:T(8,128)(2,1)S(1)} fusion(bf16[1,256,1024]{2,1,0:T(8,128)(2,1)} %bitcast.8, bf16[1,256,1024]{2,1,0:T(8,128)(2,1)} %bitcast.7, bf16[1,256,1024]{2,1,0:T(8,128)(2,1)} %bitcast.6, bf16[1,256,1024]{2,1,0:T(8,128)(2,1)S(1)} %multiply_bitcast_fusion), kind=kLoop, calls=%fused_computation | loop fusion | flops 3145728 | bytes 4194304 | tf_op jit(solution)/shard_map/stack | solution.py:201
  13.5 0.6 collective-permute-done.1.refs_1_
  14.1 0.0 copy-done
  14.1 4.2 %collective-permute-start.6 = (bf16[256,1024]{1,0:T(8,128)(2,1)S(1)}, bf16[256,1024]{1,0:T(8,128)(2,1)S(1)}, u32[]{:S(2)}, u32[]{:S(2)}) collective-permute-start(bf16[256,1024]{1,0:T(8,128)(2,1)S(1)} %copy-done), channel_id=1, source_target_pairs={{2,4},{6,8},{10,12},{14,16},{18,20},{22,24},{26,28},{30,32},{34,36... | collective-permute-start | bytes 1572872 | tf_op jit(solution)/shard_map/ppermute | solution.py:192
  18.3 0.0 collective-permute-done.4.refs_4_
  18.3 0.0 collective-permute-start.9
  18.3 4.1 %collective-permute-done.2.refs_2_ = bf16[256,1024]{1,0:T(8,128)(2,1)S(1)} collective-permute-done((bf16[256,1024]{1,0:T(8,128)(2,1)}, bf16[256,1024]{1,0:T(8,128)(2,1)S(1)}, u32[]{:S(2)}, u32[]{:S(2)}) %collective-permute-start.2) | collective-permute-done | bytes 524320 | tf_op jit(solution)/shard_map/ppermute | solution.py:186
  22.4 8.7 %collective-permute-start.8 = (bf16[256,1024]{1,0:T(8,128)(2,1)S(1)}, bf16[256,1024]{1,0:T(8,128)(2,1)S(1)}, u32[]{:S(2)}, u32[]{:S(2)}) collective-permute-start(bf16[256,1024]{1,0:T(8,128)(2,1)S(1)} %copy-done), channel_id=1, source_target_pairs={{0,64},{2,66},{4,68},{6,70},{8,72},{10,74},{12,76},{14,78},{16,80}... | collective-permute-start | bytes 1572872 | tf_op jit(solution)/shard_map/ppermute | solution.py:190
  31.1 1.0 collective-permute-done.refs_0_
  32.1 1.0 collective-permute-start.5
  33.1 1.7 %collective-permute-done.3.refs_3_ = bf16[256,1024]{1,0:T(8,128)(2,1)S(1)} collective-permute-done((bf16[256,1024]{1,0:T(8,128)(2,1)}, bf16[256,1024]{1,0:T(8,128)(2,1)S(1)}, u32[]{:S(2)}, u32[]{:S(2)}) %collective-permute-start.3) | collective-permute-done | bytes 524320 | tf_op jit(solution)/shard_map/ppermute | solution.py:190
  34.8 1.5 %collective-permute-start.7 = (bf16[256,1024]{1,0:T(8,128)(2,1)S(1)}, bf16[256,1024]{1,0:T(8,128)(2,1)S(1)}, u32[]{:S(2)}, u32[]{:S(2)}) collective-permute-start(bf16[256,1024]{1,0:T(8,128)(2,1)S(1)} %copy-done), channel_id=1, source_target_pairs={{0,1},{1,0},{2,3},{3,2},{4,5},{5,4},{6,7},{7,6},{8,9},{9,8},{10,11... | collective-permute-start | bytes 1572872 | tf_op jit(solution)/shard_map/ppermute | solution.py:186
  36.3 13.5 %probs_pass.1 = (bf16[16,256,1536]{2,1,0:T(8,128)(2,1)S(1)}, bf16[256,1024]{1,0:T(8,128)(2,1)S(1)}, f32[256,1024]{1,0:T(8,128)S(1)}, bf16[256,1024]{1,0:T(8,128)...) custom-call(s32[2,6,2]{2,1,0:T(8,128)S(1)} %copy.14.pattern, ...), custom_call_target="tpu_custom_call" | custom-call | flops 12884901888 | bytes 25165824 | tf_op jit(solution)/shard_map/probs_pass/pallas_call | solution.py:142
  49.8 0.0 collective-permute-done.6.refs_6_
  49.8 7.0 %collective-permute-start.12 = (bf16[256,1024]{1,0:T(8,128)(2,1)S(1)}, bf16[256,1024]{1,0:T(8,128)(2,1)S(1)}, u32[]{:S(2)}, u32[]{:S(2)}) collective-permute-start(bf16[256,1024]{1,0:T(8,128)(2,1)S(1)} %get-tuple-element.40), channel_id=1, source_target_pairs={{0,64},{2,66},{4,68},{6,70},{8,72},{10,74},{12,76},{14,78},{16,80}... | collective-permute-start | bytes 1572872 | tf_op jit(solution)/shard_map/ppermute | solution.py:190
  56.8 0.0 collective-permute-done.9.refs_9_
  56.8 0.0 collective-permute-start.16
  56.9 0.0 collective-permute-done.7.refs_7_
  56.9 0.1 collective-permute-start.18
  57.0 22.7 %collective-permute-done.8.refs_8_ = bf16[256,1024]{1,0:T(8,128)(2,1)S(1)} collective-permute-done((bf16[256,1024]{1,0:T(8,128)(2,1)S(1)}, bf16[256,1024]{1,0:T(8,128)(2,1)S(1)}, u32[]{:S(2)}, u32[]{:S(2)}) %collective-permute-start.8) | collective-permute-done | bytes 524320 | tf_op jit(solution)/shard_map/ppermute | solution.py:190
  79.7 2.3 %collective-permute-start.11 = (bf16[256,1024]{1,0:T(8,128)(2,1)S(1)}, bf16[256,1024]{1,0:T(8,128)(2,1)S(1)}, u32[]{:S(2)}, u32[]{:S(2)}) collective-permute-start(bf16[256,1024]{1,0:T(8,128)(2,1)S(1)} %get-tuple-element.39), channel_id=1, source_target_pairs={{0,192},{2,194},{4,196},{6,198},{8,200},{10,202},{12,204},{14,206}... | collective-permute-start | bytes 1572872 | tf_op jit(solution)/shard_map/ppermute | solution.py:190
  82.0 0.0 collective-permute-done.5.refs_5_
  82.0 0.0 collective-permute-start.19
  82.1 15.1 %grads_pass.1 = (bf16[256,1024]{1,0:T(8,128)(2,1)S(1)}, bf16[256,1024]{1,0:T(8,128)(2,1)S(1)}, bf16[256,1024]{1,0:T(8,128)(2,1)S(1)}, bf16[256,1024]{1,0:T(8,128...) custom-call(bf16[4,256,1024]{2,1,0:T(8,128)(2,1)S(1)} %pad_maximum_f, ...), custom_call_target="tpu_custom_call" | custom-call | flops 19327352832 | bytes 25165824 | tf_op jit(solution)/shard_map/grads_pass/pallas_call | solution.py:164
  97.2 0.0 collective-permute-done.16
  97.2 2.8 %collective-permute-start.17 = (bf16[256,1024]{1,0:T(8,128)(2,1)S(1)}, bf16[256,1024]{1,0:T(8,128)(2,1)S(1)}, u32[]{:S(2)}, u32[]{:S(2)}) collective-permute-start(bf16[256,1024]{1,0:T(8,128)(2,1)S(1)} %get-tuple-element.47), channel_id=1, source_target_pairs={{0,192},{2,194},{4,196},{6,198},{8,200},{10,202},{12,204},{14,206}... | collective-permute-start | bytes 1572872 | tf_op jit(solution)/shard_map/ppermute | solution.py:190
  100.0 0.0 collective-permute-done.12
  100.0 0.0 collective-permute-start.10
  100.0 2.1 %collective-permute-done.11 = bf16[256,1024]{1,0:T(8,128)(2,1)S(1)} collective-permute-done((bf16[256,1024]{1,0:T(8,128)(2,1)S(1)}, bf16[256,1024]{1,0:T(8,128)(2,1)S(1)}, u32[]{:S(2)}, u32[]{:S(2)}) %collective-permute-start.11) | collective-permute-done | bytes 524320 | tf_op jit(solution)/shard_map/ppermute | solution.py:190
  102.0 1.5 %collective-permute-start.15 = (bf16[256,1024]{1,0:T(8,128)(2,1)S(1)}, bf16[256,1024]{1,0:T(8,128)(2,1)S(1)}, u32[]{:S(2)}, u32[]{:S(2)}) collective-permute-start(bf16[256,1024]{1,0:T(8,128)(2,1)S(1)} %get-tuple-element.44), channel_id=1, source_target_pairs={{0,1},{1,0},{2,3},{3,2},{4,5},{5,4},{6,7},{7,6},{8,9},{9,8},{10,11... | collective-permute-start | bytes 1572872 | tf_op jit(solution)/shard_map/ppermute | solution.py:186
  103.5 0.0 collective-permute-done.18
  103.5 0.0 collective-permute-start.13
  103.5 0.0 collective-permute-done.19
  103.5 5.4 %collective-permute-start.14 = (bf16[256,1024]{1,0:T(8,128)(2,1)S(1)}, bf16[256,1024]{1,0:T(8,128)(2,1)S(1)}, u32[]{:S(2)}, u32[]{:S(2)}) collective-permute-start(bf16[256,1024]{1,0:T(8,128)(2,1)S(1)} %get-tuple-element.43), channel_id=1, source_target_pairs={{2,4},{6,8},{10,12},{14,16},{18,20},{22,24},{26,28},{30,32},{34,36... | collective-permute-start | bytes 1572872 | tf_op jit(solution)/shard_map/ppermute | solution.py:192
  108.9 0.8 copy.15
  109.7 0.8 copy.16
  110.5 1.4 %add_convert_fusion = bf16[256,1024]{1,0:T(8,128)(2,1)} fusion(bf16[256,1024]{1,0:T(8,128)(2,1)S(1)} %collective-permute-done.12, bf16[256,1024]{1,0:T(8,128)(2,1)S(1)} %collective-permute-done.19, bf16[256,1024]{1,0:T(8,128)(2,1)S(1)} %collective-permute-done.11, bf16[256,1024]{1,0:T(8,128)(2,1)S(1)} %collective-permute-done.18, ...), kind=kLoop, calls=%fused_computation.1 | loop fusion | flops 3145728 | bytes 3670016 | tf_op jit(solution)/shard_map/convert_element_type | solution.py:220
  111.9 0.0 collective-permute-done.17
  111.9 2.6 %collective-permute-done.10 = bf16[256,1024]{1,0:T(8,128)(2,1)S(1)} collective-permute-done((bf16[256,1024]{1,0:T(8,128)(2,1)S(1)}, bf16[256,1024]{1,0:T(8,128)(2,1)S(1)}, u32[]{:S(2)}, u32[]{:S(2)}) %collective-permute-start.10) | collective-permute-done | bytes 524320 | tf_op jit(solution)/shard_map/ppermute | solution.py:190
  114.4 0.5 collective-permute-done.15
  115.0 0.0 collective-permute-done.13
  115.0 7.4 %collective-permute-done.14 = bf16[256,1024]{1,0:T(8,128)(2,1)S(1)} collective-permute-done((bf16[256,1024]{1,0:T(8,128)(2,1)S(1)}, bf16[256,1024]{1,0:T(8,128)(2,1)S(1)}, u32[]{:S(2)}, u32[]{:S(2)}) %collective-permute-start.14) | collective-permute-done | bytes 524320 | tf_op jit(solution)/shard_map/ppermute | solution.py:192
  122.3 1.4 %add_convert_fusion.1 = bf16[256,1024]{1,0:T(8,128)(2,1)} fusion(bf16[256,1024]{1,0:T(8,128)(2,1)S(1)} %collective-permute-done.17, bf16[256,1024]{1,0:T(8,128)(2,1)S(1)} %collective-permute-done.15, bf16[256,1024]{1,0:T(8,128)(2,1)S(1)} %collective-permute-done.14, bf16[256,1024]{1,0:T(8,128)(2,1)S(1)} %collective-permute-done.13, ...), kind=kLoop, calls=%fused_computation.2 | loop fusion | flops 3145728 | bytes 3670016 | tf_op jit(solution)/shard_map/convert_element_type | solution.py:229
Async XLA Ops:
  0.6 13.5 %collective-permute-start.1 = (bf16[256,1024]{1,0:T(8,128)(2,1)}, bf16[256,1024]{1,0:T(8,128)(2,1)S(1)}, u32[]{:S(2)}, u32[]{:S(2)}) collective-permute-start(bf16[256,1024]{1,0:T(8,128)(2,1)} %param.6), channel_id=1, source_target_pairs={{2,4},{6,8},{10,12},{14,16},{18,20},{22,24},{26,28},{30,32},{34,36... | collective-permute-start | bytes 1572872 | tf_op jit(solution)/shard_map/ppermute | solution.py:192
  2.5 15.7 %collective-permute-start.4 = (bf16[256,1024]{1,0:T(8,128)(2,1)}, bf16[256,1024]{1,0:T(8,128)(2,1)S(1)}, u32[]{:S(2)}, u32[]{:S(2)}) collective-permute-start(bf16[256,1024]{1,0:T(8,128)(2,1)} %param.6), channel_id=1, source_target_pairs={{0,2},{4,6},{8,10},{12,14},{16,18},{20,22},{24,26},{28,30},{32,34}... | collective-permute-start | bytes 1572872 | tf_op jit(solution)/shard_map/ppermute | solution.py:192
  2.5 19.9 %collective-permute-start.2 = (bf16[256,1024]{1,0:T(8,128)(2,1)}, bf16[256,1024]{1,0:T(8,128)(2,1)S(1)}, u32[]{:S(2)}, u32[]{:S(2)}) collective-permute-start(bf16[256,1024]{1,0:T(8,128)(2,1)} %param.6), channel_id=1, source_target_pairs={{0,1},{1,0},{2,3},{3,2},{4,5},{5,4},{6,7},{7,6},{8,9},{9,8},{10,11... | collective-permute-start | bytes 1572872 | tf_op jit(solution)/shard_map/ppermute | solution.py:186
  4.7 27.4 %collective-permute-start = (bf16[256,1024]{1,0:T(8,128)(2,1)}, bf16[256,1024]{1,0:T(8,128)(2,1)S(1)}, u32[]{:S(2)}, u32[]{:S(2)}) collective-permute-start(bf16[256,1024]{1,0:T(8,128)(2,1)} %param.6), channel_id=1, source_target_pairs={{0,192},{2,194},{4,196},{6,198},{8,200},{10,202},{12,204},{14,206}... | collective-permute-start | bytes 1572872 | tf_op jit(solution)/shard_map/ppermute | solution.py:190
  8.5 26.3 %collective-permute-start.3 = (bf16[256,1024]{1,0:T(8,128)(2,1)}, bf16[256,1024]{1,0:T(8,128)(2,1)S(1)}, u32[]{:S(2)}, u32[]{:S(2)}) collective-permute-start(bf16[256,1024]{1,0:T(8,128)(2,1)} %param.6), channel_id=1, source_target_pairs={{0,64},{2,66},{4,68},{6,70},{8,72},{10,74},{12,76},{14,78},{16,80}... | collective-permute-start | bytes 1572872 | tf_op jit(solution)/shard_map/ppermute | solution.py:190
  11.8 2.3 %copy-start = (bf16[256,1024]{1,0:T(8,128)(2,1)S(1)}, bf16[256,1024]{1,0:T(8,128)(2,1)}, u32[]{:S(2)}) copy-start(bf16[256,1024]{1,0:T(8,128)(2,1)} %param.7) | copy-start | bytes 1572868
  14.1 35.7 %collective-permute-start.6 = (bf16[256,1024]{1,0:T(8,128)(2,1)S(1)}, bf16[256,1024]{1,0:T(8,128)(2,1)S(1)}, u32[]{:S(2)}, u32[]{:S(2)}) collective-permute-start(bf16[256,1024]{1,0:T(8,128)(2,1)S(1)} %copy-done), channel_id=1, source_target_pairs={{2,4},{6,8},{10,12},{14,16},{18,20},{22,24},{26,28},{30,32},{34,36... | collective-permute-start | bytes 1572872 | tf_op jit(solution)/shard_map/ppermute | solution.py:192
  18.3 38.6 %collective-permute-start.9 = (bf16[256,1024]{1,0:T(8,128)(2,1)S(1)}, bf16[256,1024]{1,0:T(8,128)(2,1)S(1)}, u32[]{:S(2)}, u32[]{:S(2)}) collective-permute-start(bf16[256,1024]{1,0:T(8,128)(2,1)S(1)} %copy-done), channel_id=1, source_target_pairs={{0,2},{4,6},{8,10},{12,14},{16,18},{20,22},{24,26},{28,30},{32,34}... | collective-permute-start | bytes 1572872 | tf_op jit(solution)/shard_map/ppermute | solution.py:192
  22.4 57.3 %collective-permute-start.8 = (bf16[256,1024]{1,0:T(8,128)(2,1)S(1)}, bf16[256,1024]{1,0:T(8,128)(2,1)S(1)}, u32[]{:S(2)}, u32[]{:S(2)}) collective-permute-start(bf16[256,1024]{1,0:T(8,128)(2,1)S(1)} %copy-done), channel_id=1, source_target_pairs={{0,64},{2,66},{4,68},{6,70},{8,72},{10,74},{12,76},{14,78},{16,80}... | collective-permute-start | bytes 1572872 | tf_op jit(solution)/shard_map/ppermute | solution.py:190
  32.1 49.9 %collective-permute-start.5 = (bf16[256,1024]{1,0:T(8,128)(2,1)S(1)}, bf16[256,1024]{1,0:T(8,128)(2,1)S(1)}, u32[]{:S(2)}, u32[]{:S(2)}) collective-permute-start(bf16[256,1024]{1,0:T(8,128)(2,1)S(1)} %copy-done), channel_id=1, source_target_pairs={{0,192},{2,194},{4,196},{6,198},{8,200},{10,202},{12,204},{14,206}... | collective-permute-start | bytes 1572872 | tf_op jit(solution)/shard_map/ppermute | solution.py:190
  34.8 22.0 %collective-permute-start.7 = (bf16[256,1024]{1,0:T(8,128)(2,1)S(1)}, bf16[256,1024]{1,0:T(8,128)(2,1)S(1)}, u32[]{:S(2)}, u32[]{:S(2)}) collective-permute-start(bf16[256,1024]{1,0:T(8,128)(2,1)S(1)} %copy-done), channel_id=1, source_target_pairs={{0,1},{1,0},{2,3},{3,2},{4,5},{5,4},{6,7},{7,6},{8,9},{9,8},{10,11... | collective-permute-start | bytes 1572872 | tf_op jit(solution)/shard_map/ppermute | solution.py:186
  49.8 50.2 %collective-permute-start.12 = (bf16[256,1024]{1,0:T(8,128)(2,1)S(1)}, bf16[256,1024]{1,0:T(8,128)(2,1)S(1)}, u32[]{:S(2)}, u32[]{:S(2)}) collective-permute-start(bf16[256,1024]{1,0:T(8,128)(2,1)S(1)} %get-tuple-element.40), channel_id=1, source_target_pairs={{0,64},{2,66},{4,68},{6,70},{8,72},{10,74},{12,76},{14,78},{16,80}... | collective-permute-start | bytes 1572872 | tf_op jit(solution)/shard_map/ppermute | solution.py:190
  56.8 40.3 %collective-permute-start.16 = (bf16[256,1024]{1,0:T(8,128)(2,1)S(1)}, bf16[256,1024]{1,0:T(8,128)(2,1)S(1)}, u32[]{:S(2)}, u32[]{:S(2)}) collective-permute-start(bf16[256,1024]{1,0:T(8,128)(2,1)S(1)} %get-tuple-element.46), channel_id=1, source_target_pairs={{0,1},{1,0},{2,3},{3,2},{4,5},{5,4},{6,7},{7,6},{8,9},{9,8},{10,11... | collective-permute-start | bytes 1572872 | tf_op jit(solution)/shard_map/ppermute | solution.py:186
  56.9 46.7 %collective-permute-start.18 = (bf16[256,1024]{1,0:T(8,128)(2,1)S(1)}, bf16[256,1024]{1,0:T(8,128)(2,1)S(1)}, u32[]{:S(2)}, u32[]{:S(2)}) collective-permute-start(bf16[256,1024]{1,0:T(8,128)(2,1)S(1)} %get-tuple-element.49), channel_id=1, source_target_pairs={{0,2},{4,6},{8,10},{12,14},{16,18},{20,22},{24,26},{28,30},{32,34}... | collective-permute-start | bytes 1572872 | tf_op jit(solution)/shard_map/ppermute | solution.py:192
  79.7 22.3 %collective-permute-start.11 = (bf16[256,1024]{1,0:T(8,128)(2,1)S(1)}, bf16[256,1024]{1,0:T(8,128)(2,1)S(1)}, u32[]{:S(2)}, u32[]{:S(2)}) collective-permute-start(bf16[256,1024]{1,0:T(8,128)(2,1)S(1)} %get-tuple-element.39), channel_id=1, source_target_pairs={{0,192},{2,194},{4,196},{6,198},{8,200},{10,202},{12,204},{14,206}... | collective-permute-start | bytes 1572872 | tf_op jit(solution)/shard_map/ppermute | solution.py:190
  82.0 21.5 %collective-permute-start.19 = (bf16[256,1024]{1,0:T(8,128)(2,1)S(1)}, bf16[256,1024]{1,0:T(8,128)(2,1)S(1)}, u32[]{:S(2)}, u32[]{:S(2)}) collective-permute-start(bf16[256,1024]{1,0:T(8,128)(2,1)S(1)} %get-tuple-element.51), channel_id=1, source_target_pairs={{2,4},{6,8},{10,12},{14,16},{18,20},{22,24},{26,28},{30,32},{34,36... | collective-permute-start | bytes 1572872 | tf_op jit(solution)/shard_map/ppermute | solution.py:192
  97.2 14.7 %collective-permute-start.17 = (bf16[256,1024]{1,0:T(8,128)(2,1)S(1)}, bf16[256,1024]{1,0:T(8,128)(2,1)S(1)}, u32[]{:S(2)}, u32[]{:S(2)}) collective-permute-start(bf16[256,1024]{1,0:T(8,128)(2,1)S(1)} %get-tuple-element.47), channel_id=1, source_target_pairs={{0,192},{2,194},{4,196},{6,198},{8,200},{10,202},{12,204},{14,206}... | collective-permute-start | bytes 1572872 | tf_op jit(solution)/shard_map/ppermute | solution.py:190
  100.0 14.5 %collective-permute-start.10 = (bf16[256,1024]{1,0:T(8,128)(2,1)S(1)}, bf16[256,1024]{1,0:T(8,128)(2,1)S(1)}, u32[]{:S(2)}, u32[]{:S(2)}) collective-permute-start(bf16[256,1024]{1,0:T(8,128)(2,1)S(1)} %get-tuple-element.36), channel_id=1, source_target_pairs={{0,64},{2,66},{4,68},{6,70},{8,72},{10,74},{12,76},{14,78},{16,80}... | collective-permute-start | bytes 1572872 | tf_op jit(solution)/shard_map/ppermute | solution.py:190
  102.0 12.9 %collective-permute-start.15 = (bf16[256,1024]{1,0:T(8,128)(2,1)S(1)}, bf16[256,1024]{1,0:T(8,128)(2,1)S(1)}, u32[]{:S(2)}, u32[]{:S(2)}) collective-permute-start(bf16[256,1024]{1,0:T(8,128)(2,1)S(1)} %get-tuple-element.44), channel_id=1, source_target_pairs={{0,1},{1,0},{2,3},{3,2},{4,5},{5,4},{6,7},{7,6},{8,9},{9,8},{10,11... | collective-permute-start | bytes 1572872 | tf_op jit(solution)/shard_map/ppermute | solution.py:186
  103.5 11.4 %collective-permute-start.13 = (bf16[256,1024]{1,0:T(8,128)(2,1)S(1)}, bf16[256,1024]{1,0:T(8,128)(2,1)S(1)}, u32[]{:S(2)}, u32[]{:S(2)}) collective-permute-start(bf16[256,1024]{1,0:T(8,128)(2,1)S(1)} %get-tuple-element.41), channel_id=1, source_target_pairs={{0,2},{4,6},{8,10},{12,14},{16,18},{20,22},{24,26},{28,30},{32,34}... | collective-permute-start | bytes 1572872 | tf_op jit(solution)/shard_map/ppermute | solution.py:192
  103.5 18.8 %collective-permute-start.14 = (bf16[256,1024]{1,0:T(8,128)(2,1)S(1)}, bf16[256,1024]{1,0:T(8,128)(2,1)S(1)}, u32[]{:S(2)}, u32[]{:S(2)}) collective-permute-start(bf16[256,1024]{1,0:T(8,128)(2,1)S(1)} %get-tuple-element.43), channel_id=1, source_target_pairs={{2,4},{6,8},{10,12},{14,16},{18,20},{22,24},{26,28},{30,32},{34,36... | collective-permute-start | bytes 1572872 | tf_op jit(solution)/shard_map/ppermute | solution.py:192

commit v4 on v3

--- a/solution.py
+++ b/solution.py
@@ -221,7 +221,7 @@
     attended, grad_query, terms = grads_pass(own, scaled, inv, probs, keys, values)
     terms = dict(zip(SOURCES, terms))
     back2 = dict(own=terms["own"])
-    for n, deps in [['below', ['half']], ['half', []], ['pair', ['below']], ['chip', ['below', 'above']], ['above', []]]:
+    for n, deps in [['below', ['half']], ['half', []], ['pair', []], ['chip', ['below', 'above']], ['above', []]]:
         back2[n] = move(after(terms[n], *[back[d] for d in deps]), n, -1)
     total = back2["own"].astype(f32)
     for n in ['above', 'chip', 'pair', 'half', 'below']:

time: 126 us -> 125 us (level)
  transfers between devices with their start and end apart: 20 -> 20, of which waited for: 9 -> 8; matrix products, arithmetic and copies ran while one was open for 6% -> 6% of each run, Pallas kernels for 23% -> 23%
where the time goes in v4:
time: 125 us; the launch traced here: 124 us
  waiting for transfers between devices  43.8 us (35%)
  starting transfers between devices  41.8 us (33%)
  Pallas kernels  28.5 us (23%)
  other arithmetic  5.58 us (4%)
  local copies, waits for them, and re-layouts  3.37 us (3%)
    ppermute x8, waiting for transfers between devices, move(): lax.ppermute(x, 'gx', [(i, (i + reach) % peers) for i in range(peers)])  31.1 us
    ppermute x8, starting transfers between devices, move(): lax.ppermute(x, 'gx', [(i, (i + reach) % peers) for i in range(peers)])  26 us
    pallas_call x1, Pallas kernels, grads_pass(): pl.pallas_call(grads_kernel, grid=(PAIRS,), in_specs=[whole] * (2 + 2 * N...  15.1 us
    pallas_call x1, Pallas kernels, probs_pass(): pl.pallas_call(probs_kernel, grid=(PAIRS,), in_specs=[pl.BlockSpec(memory...  13.5 us
    ppermute x8, starting transfers between devices, move(): return lax.ppermute(x, 'gx', ends + [(b, a) for a, b in ends])  10.4 us
    ppermute x8, waiting for transfers between devices, move(): return lax.ppermute(x, 'gx', ends + [(b, a) for a, b in ends])  8.52 us
    ppermute x4, starting transfers between devices, move(): return lax.ppermute(x, 'gz', [(0, 1), (1, 0)])  5.39 us
    ppermute x4, waiting for transfers between devices, move(): return lax.ppermute(x, 'gz', [(0, 1), (1, 0)])  4.15 us
  transfers between devices with their start and end apart: 20, of which 8 were waited for; matrix products, arithmetic and copies ran while one was open for 6% of the time, Pallas kernels for 23%

profile of v4, /device:TPU:59, one launch (start us, length us, event | category | flops | bytes accessed | tf_op | source)
XLA Modules:
  0.0 123.7 jit_solution(6783367267904729639)
XLA Ops:
  0.6 1.9 %collective-permute-start.1 = (bf16[256,1024]{1,0:T(8,128)(2,1)}, bf16[256,1024]{1,0:T(8,128)(2,1)S(1)}, u32[]{:S(2)}, u32[]{:S(2)}) collective-permute-start(bf16[256,1024]{1,0:T(8,128)(2,1)} %param.6), channel_id=1, source_target_pairs={{2,4},{6,8},{10,12},{14,16},{18,20},{22,24},{26,28},{30,32},{34,36... | collective-permute-start | bytes 1572872 | tf_op jit(solution)/shard_map/ppermute | solution.py:192
  2.5 0.0 collective-permute-start.4
  2.5 2.1 %collective-permute-start.2 = (bf16[256,1024]{1,0:T(8,128)(2,1)}, bf16[256,1024]{1,0:T(8,128)(2,1)S(1)}, u32[]{:S(2)}, u32[]{:S(2)}) collective-permute-start(bf16[256,1024]{1,0:T(8,128)(2,1)} %param.6), channel_id=1, source_target_pairs={{0,1},{1,0},{2,3},{3,2},{4,5},{5,4},{6,7},{7,6},{8,9},{9,8},{10,11... | collective-permute-start | bytes 1572872 | tf_op jit(solution)/shard_map/ppermute | solution.py:186
  4.7 3.9 %collective-permute-start = (bf16[256,1024]{1,0:T(8,128)(2,1)}, bf16[256,1024]{1,0:T(8,128)(2,1)S(1)}, u32[]{:S(2)}, u32[]{:S(2)}) collective-permute-start(bf16[256,1024]{1,0:T(8,128)(2,1)} %param.6), channel_id=1, source_target_pairs={{0,192},{2,194},{4,196},{6,198},{8,200},{10,202},{12,204},{14,206}... | collective-permute-start | bytes 1572872 | tf_op jit(solution)/shard_map/ppermute | solution.py:190
  8.5 0.4 collective-permute-start.3
  8.9 0.9 constant_dynamic-slice_fusion
  9.8 0.8 stack.29
  10.6 0.1 copy.14.pattern
  10.7 1.1 multiply_bitcast_fusion
  11.8 0.0 copy-start
  11.8 1.7 %pad_maximum_fusion.own_ref = bf16[4,256,1024]{2,1,0:T(8,128)(2,1)S(1)} fusion(bf16[1,256,1024]{2,1,0:T(8,128)(2,1)} %bitcast.8, bf16[1,256,1024]{2,1,0:T(8,128)(2,1)} %bitcast.7, bf16[1,256,1024]{2,1,0:T(8,128)(2,1)} %bitcast.6, bf16[1,256,1024]{2,1,0:T(8,128)(2,1)S(1)} %multiply_bitcast_fusion), kind=kLoop, calls=%fused_computation | loop fusion | flops 3145728 | bytes 4194304 | tf_op jit(solution)/shard_map/stack | solution.py:201
  13.5 0.6 collective-permute-done.1.refs_1_
  14.1 0.0 copy-done
  14.1 4.2 %collective-permute-start.6 = (bf16[256,1024]{1,0:T(8,128)(2,1)S(1)}, bf16[256,1024]{1,0:T(8,128)(2,1)S(1)}, u32[]{:S(2)}, u32[]{:S(2)}) collective-permute-start(bf16[256,1024]{1,0:T(8,128)(2,1)S(1)} %copy-done), channel_id=1, source_target_pairs={{2,4},{6,8},{10,12},{14,16},{18,20},{22,24},{26,28},{30,32},{34,36... | collective-permute-start | bytes 1572872 | tf_op jit(solution)/shard_map/ppermute | solution.py:192
  18.3 0.0 collective-permute-done.4.refs_4_
  18.3 0.0 collective-permute-start.9
  18.3 4.1 %collective-permute-done.2.refs_2_ = bf16[256,1024]{1,0:T(8,128)(2,1)S(1)} collective-permute-done((bf16[256,1024]{1,0:T(8,128)(2,1)}, bf16[256,1024]{1,0:T(8,128)(2,1)S(1)}, u32[]{:S(2)}, u32[]{:S(2)}) %collective-permute-start.2) | collective-permute-done | bytes 524320 | tf_op jit(solution)/shard_map/ppermute | solution.py:186
  22.4 8.7 %collective-permute-start.8 = (bf16[256,1024]{1,0:T(8,128)(2,1)S(1)}, bf16[256,1024]{1,0:T(8,128)(2,1)S(1)}, u32[]{:S(2)}, u32[]{:S(2)}) collective-permute-start(bf16[256,1024]{1,0:T(8,128)(2,1)S(1)} %copy-done), channel_id=1, source_target_pairs={{0,64},{2,66},{4,68},{6,70},{8,72},{10,74},{12,76},{14,78},{16,80}... | collective-permute-start | bytes 1572872 | tf_op jit(solution)/shard_map/ppermute | solution.py:190
  31.1 1.0 collective-permute-done.refs_0_
  32.1 1.0 collective-permute-start.5
  33.1 1.7 %collective-permute-done.3.refs_3_ = bf16[256,1024]{1,0:T(8,128)(2,1)S(1)} collective-permute-done((bf16[256,1024]{1,0:T(8,128)(2,1)}, bf16[256,1024]{1,0:T(8,128)(2,1)S(1)}, u32[]{:S(2)}, u32[]{:S(2)}) %collective-permute-start.3) | collective-permute-done | bytes 524320 | tf_op jit(solution)/shard_map/ppermute | solution.py:190
  34.8 1.5 %collective-permute-start.7 = (bf16[256,1024]{1,0:T(8,128)(2,1)S(1)}, bf16[256,1024]{1,0:T(8,128)(2,1)S(1)}, u32[]{:S(2)}, u32[]{:S(2)}) collective-permute-start(bf16[256,1024]{1,0:T(8,128)(2,1)S(1)} %copy-done), channel_id=1, source_target_pairs={{0,1},{1,0},{2,3},{3,2},{4,5},{5,4},{6,7},{7,6},{8,9},{9,8},{10,11... | collective-permute-start | bytes 1572872 | tf_op jit(solution)/shard_map/ppermute | solution.py:186
  36.3 13.5 %probs_pass.1 = (bf16[16,256,1536]{2,1,0:T(8,128)(2,1)S(1)}, bf16[256,1024]{1,0:T(8,128)(2,1)S(1)}, f32[256,1024]{1,0:T(8,128)S(1)}, bf16[256,1024]{1,0:T(8,128)...) custom-call(s32[2,6,2]{2,1,0:T(8,128)S(1)} %copy.14.pattern, ...), custom_call_target="tpu_custom_call" | custom-call | flops 12884901888 | bytes 25165824 | tf_op jit(solution)/shard_map/probs_pass/pallas_call | solution.py:142
  49.8 0.0 collective-permute-done.6.refs_6_
  49.8 7.0 %collective-permute-start.12 = (bf16[256,1024]{1,0:T(8,128)(2,1)S(1)}, bf16[256,1024]{1,0:T(8,128)(2,1)S(1)}, u32[]{:S(2)}, u32[]{:S(2)}) collective-permute-start(bf16[256,1024]{1,0:T(8,128)(2,1)S(1)} %get-tuple-element.39), channel_id=1, source_target_pairs={{0,64},{2,66},{4,68},{6,70},{8,72},{10,74},{12,76},{14,78},{16,80}... | collective-permute-start | bytes 1572872 | tf_op jit(solution)/shard_map/ppermute | solution.py:190
  56.8 0.0 collective-permute-done.9.refs_9_
  56.8 0.0 collective-permute-start.16
  56.9 0.0 collective-permute-done.7.refs_7_
  56.9 0.1 collective-permute-start.18
  57.0 22.7 %collective-permute-done.8.refs_8_ = bf16[256,1024]{1,0:T(8,128)(2,1)S(1)} collective-permute-done((bf16[256,1024]{1,0:T(8,128)(2,1)S(1)}, bf16[256,1024]{1,0:T(8,128)(2,1)S(1)}, u32[]{:S(2)}, u32[]{:S(2)}) %collective-permute-start.8) | collective-permute-done | bytes 524320 | tf_op jit(solution)/shard_map/ppermute | solution.py:190
  79.7 2.3 %collective-permute-start.11 = (bf16[256,1024]{1,0:T(8,128)(2,1)S(1)}, bf16[256,1024]{1,0:T(8,128)(2,1)S(1)}, u32[]{:S(2)}, u32[]{:S(2)}) collective-permute-start(bf16[256,1024]{1,0:T(8,128)(2,1)S(1)} %get-tuple-element.38), channel_id=1, source_target_pairs={{0,192},{2,194},{4,196},{6,198},{8,200},{10,202},{12,204},{14,206}... | collective-permute-start | bytes 1572872 | tf_op jit(solution)/shard_map/ppermute | solution.py:190
  82.0 0.0 collective-permute-done.5.refs_5_
  82.0 0.0 collective-permute-start.19
  82.1 15.1 %grads_pass.1 = (bf16[256,1024]{1,0:T(8,128)(2,1)S(1)}, bf16[256,1024]{1,0:T(8,128)(2,1)S(1)}, bf16[256,1024]{1,0:T(8,128)(2,1)S(1)}, bf16[256,1024]{1,0:T(8,128...) custom-call(bf16[4,256,1024]{2,1,0:T(8,128)(2,1)S(1)} %pad_maximum_f, ...), custom_call_target="tpu_custom_call" | custom-call | flops 19327352832 | bytes 25165824 | tf_op jit(solution)/shard_map/grads_pass/pallas_call | solution.py:164
  97.2 0.0 collective-permute-done.16
  97.2 2.8 %collective-permute-start.17 = (bf16[256,1024]{1,0:T(8,128)(2,1)S(1)}, bf16[256,1024]{1,0:T(8,128)(2,1)S(1)}, u32[]{:S(2)}, u32[]{:S(2)}) collective-permute-start(bf16[256,1024]{1,0:T(8,128)(2,1)S(1)} %get-tuple-element.45), channel_id=1, source_target_pairs={{0,192},{2,194},{4,196},{6,198},{8,200},{10,202},{12,204},{14,206}... | collective-permute-start | bytes 1572872 | tf_op jit(solution)/shard_map/ppermute | solution.py:190
  100.0 0.0 collective-permute-done.12
  100.0 0.0 collective-permute-start.10
  100.0 2.1 %collective-permute-done.11 = bf16[256,1024]{1,0:T(8,128)(2,1)S(1)} collective-permute-done((bf16[256,1024]{1,0:T(8,128)(2,1)S(1)}, bf16[256,1024]{1,0:T(8,128)(2,1)S(1)}, u32[]{:S(2)}, u32[]{:S(2)}) %collective-permute-start.11) | collective-permute-done | bytes 524320 | tf_op jit(solution)/shard_map/ppermute | solution.py:190
  102.0 4.1 %collective-permute-start.14 = (bf16[256,1024]{1,0:T(8,128)(2,1)S(1)}, bf16[256,1024]{1,0:T(8,128)(2,1)S(1)}, u32[]{:S(2)}, u32[]{:S(2)}) collective-permute-start(bf16[256,1024]{1,0:T(8,128)(2,1)S(1)} %get-tuple-element.41), channel_id=1, source_target_pairs={{2,4},{6,8},{10,12},{14,16},{18,20},{22,24},{26,28},{30,32},{34,36... | collective-permute-start | bytes 1572872 | tf_op jit(solution)/shard_map/ppermute | solution.py:192
  106.1 0.0 collective-permute-done.18
  106.1 1.8 %collective-permute-start.15 = (bf16[256,1024]{1,0:T(8,128)(2,1)S(1)}, bf16[256,1024]{1,0:T(8,128)(2,1)S(1)}, u32[]{:S(2)}, u32[]{:S(2)}) collective-permute-start(bf16[256,1024]{1,0:T(8,128)(2,1)S(1)} %get-tuple-element.42), channel_id=1, source_target_pairs={{0,1},{1,0},{2,3},{3,2},{4,5},{5,4},{6,7},{7,6},{8,9},{9,8},{10,11... | collective-permute-start | bytes 1572872 | tf_op jit(solution)/shard_map/ppermute | solution.py:186
  107.9 0.0 collective-permute-done.19
  107.9 0.0 collective-permute-start.13
  107.9 0.8 copy.15
  108.7 0.8 copy.16
  109.5 1.4 %add_convert_fusion = bf16[256,1024]{1,0:T(8,128)(2,1)} fusion(bf16[256,1024]{1,0:T(8,128)(2,1)S(1)} %collective-permute-done.12, bf16[256,1024]{1,0:T(8,128)(2,1)S(1)} %collective-permute-done.19, bf16[256,1024]{1,0:T(8,128)(2,1)S(1)} %collective-permute-done.11, bf16[256,1024]{1,0:T(8,128)(2,1)S(1)} %collective-permute-done.18, ...), kind=kLoop, calls=%fused_computation.1 | loop fusion | flops 3145728 | bytes 3670016 | tf_op jit(solution)/shard_map/convert_element_type | solution.py:220
  110.9 0.0 collective-permute-done.17
  110.9 3.5 %collective-permute-done.10 = bf16[256,1024]{1,0:T(8,128)(2,1)S(1)} collective-permute-done((bf16[256,1024]{1,0:T(8,128)(2,1)S(1)}, bf16[256,1024]{1,0:T(8,128)(2,1)S(1)}, u32[]{:S(2)}, u32[]{:S(2)}) %collective-permute-start.10) | collective-permute-done | bytes 524320 | tf_op jit(solution)/shard_map/ppermute | solution.py:190
  114.4 7.9 %collective-permute-done.14 = bf16[256,1024]{1,0:T(8,128)(2,1)S(1)} collective-permute-done((bf16[256,1024]{1,0:T(8,128)(2,1)S(1)}, bf16[256,1024]{1,0:T(8,128)(2,1)S(1)}, u32[]{:S(2)}, u32[]{:S(2)}) %collective-permute-start.14) | collective-permute-done | bytes 524320 | tf_op jit(solution)/shard_map/ppermute | solution.py:192
  122.3 0.0 collective-permute-done.15
  122.3 0.0 collective-permute-done.13
  122.3 1.4 %add_convert_fusion.1 = bf16[256,1024]{1,0:T(8,128)(2,1)} fusion(bf16[256,1024]{1,0:T(8,128)(2,1)S(1)} %collective-permute-done.17, bf16[256,1024]{1,0:T(8,128)(2,1)S(1)} %collective-permute-done.15, bf16[256,1024]{1,0:T(8,128)(2,1)S(1)} %collective-permute-done.14, bf16[256,1024]{1,0:T(8,128)(2,1)S(1)} %collective-permute-done.13, ...), kind=kLoop, calls=%fused_computation.2 | loop fusion | flops 3145728 | bytes 3670016 | tf_op jit(solution)/shard_map/convert_element_type | solution.py:229
Async XLA Ops:
  0.6 13.5 %collective-permute-start.1 = (bf16[256,1024]{1,0:T(8,128)(2,1)}, bf16[256,1024]{1,0:T(8,128)(2,1)S(1)}, u32[]{:S(2)}, u32[]{:S(2)}) collective-permute-start(bf16[256,1024]{1,0:T(8,128)(2,1)} %param.6), channel_id=1, source_target_pairs={{2,4},{6,8},{10,12},{14,16},{18,20},{22,24},{26,28},{30,32},{34,36... | collective-permute-start | bytes 1572872 | tf_op jit(solution)/shard_map/ppermute | solution.py:192
  2.5 15.7 %collective-permute-start.4 = (bf16[256,1024]{1,0:T(8,128)(2,1)}, bf16[256,1024]{1,0:T(8,128)(2,1)S(1)}, u32[]{:S(2)}, u32[]{:S(2)}) collective-permute-start(bf16[256,1024]{1,0:T(8,128)(2,1)} %param.6), channel_id=1, source_target_pairs={{0,2},{4,6},{8,10},{12,14},{16,18},{20,22},{24,26},{28,30},{32,34}... | collective-permute-start | bytes 1572872 | tf_op jit(solution)/shard_map/ppermute | solution.py:192
  2.5 19.9 %collective-permute-start.2 = (bf16[256,1024]{1,0:T(8,128)(2,1)}, bf16[256,1024]{1,0:T(8,128)(2,1)S(1)}, u32[]{:S(2)}, u32[]{:S(2)}) collective-permute-start(bf16[256,1024]{1,0:T(8,128)(2,1)} %param.6), channel_id=1, source_target_pairs={{0,1},{1,0},{2,3},{3,2},{4,5},{5,4},{6,7},{7,6},{8,9},{9,8},{10,11... | collective-permute-start | bytes 1572872 | tf_op jit(solution)/shard_map/ppermute | solution.py:186
  4.7 27.4 %collective-permute-start = (bf16[256,1024]{1,0:T(8,128)(2,1)}, bf16[256,1024]{1,0:T(8,128)(2,1)S(1)}, u32[]{:S(2)}, u32[]{:S(2)}) collective-permute-start(bf16[256,1024]{1,0:T(8,128)(2,1)} %param.6), channel_id=1, source_target_pairs={{0,192},{2,194},{4,196},{6,198},{8,200},{10,202},{12,204},{14,206}... | collective-permute-start | bytes 1572872 | tf_op jit(solution)/shard_map/ppermute | solution.py:190
  8.5 26.3 %collective-permute-start.3 = (bf16[256,1024]{1,0:T(8,128)(2,1)}, bf16[256,1024]{1,0:T(8,128)(2,1)S(1)}, u32[]{:S(2)}, u32[]{:S(2)}) collective-permute-start(bf16[256,1024]{1,0:T(8,128)(2,1)} %param.6), channel_id=1, source_target_pairs={{0,64},{2,66},{4,68},{6,70},{8,72},{10,74},{12,76},{14,78},{16,80}... | collective-permute-start | bytes 1572872 | tf_op jit(solution)/shard_map/ppermute | solution.py:190
  11.8 2.3 %copy-start = (bf16[256,1024]{1,0:T(8,128)(2,1)S(1)}, bf16[256,1024]{1,0:T(8,128)(2,1)}, u32[]{:S(2)}) copy-start(bf16[256,1024]{1,0:T(8,128)(2,1)} %param.7) | copy-start | bytes 1572868
  14.1 35.7 %collective-permute-start.6 = (bf16[256,1024]{1,0:T(8,128)(2,1)S(1)}, bf16[256,1024]{1,0:T(8,128)(2,1)S(1)}, u32[]{:S(2)}, u32[]{:S(2)}) collective-permute-start(bf16[256,1024]{1,0:T(8,128)(2,1)S(1)} %copy-done), channel_id=1, source_target_pairs={{2,4},{6,8},{10,12},{14,16},{18,20},{22,24},{26,28},{30,32},{34,36... | collective-permute-start | bytes 1572872 | tf_op jit(solution)/shard_map/ppermute | solution.py:192
  18.3 38.6 %collective-permute-start.9 = (bf16[256,1024]{1,0:T(8,128)(2,1)S(1)}, bf16[256,1024]{1,0:T(8,128)(2,1)S(1)}, u32[]{:S(2)}, u32[]{:S(2)}) collective-permute-start(bf16[256,1024]{1,0:T(8,128)(2,1)S(1)} %copy-done), channel_id=1, source_target_pairs={{0,2},{4,6},{8,10},{12,14},{16,18},{20,22},{24,26},{28,30},{32,34}... | collective-permute-start | bytes 1572872 | tf_op jit(solution)/shard_map/ppermute | solution.py:192
  22.4 57.3 %collective-permute-start.8 = (bf16[256,1024]{1,0:T(8,128)(2,1)S(1)}, bf16[256,1024]{1,0:T(8,128)(2,1)S(1)}, u32[]{:S(2)}, u32[]{:S(2)}) collective-permute-start(bf16[256,1024]{1,0:T(8,128)(2,1)S(1)} %copy-done), channel_id=1, source_target_pairs={{0,64},{2,66},{4,68},{6,70},{8,72},{10,74},{12,76},{14,78},{16,80}... | collective-permute-start | bytes 1572872 | tf_op jit(solution)/shard_map/ppermute | solution.py:190
  32.1 49.9 %collective-permute-start.5 = (bf16[256,1024]{1,0:T(8,128)(2,1)S(1)}, bf16[256,1024]{1,0:T(8,128)(2,1)S(1)}, u32[]{:S(2)}, u32[]{:S(2)}) collective-permute-start(bf16[256,1024]{1,0:T(8,128)(2,1)S(1)} %copy-done), channel_id=1, source_target_pairs={{0,192},{2,194},{4,196},{6,198},{8,200},{10,202},{12,204},{14,206}... | collective-permute-start | bytes 1572872 | tf_op jit(solution)/shard_map/ppermute | solution.py:190
  34.8 22.0 %collective-permute-start.7 = (bf16[256,1024]{1,0:T(8,128)(2,1)S(1)}, bf16[256,1024]{1,0:T(8,128)(2,1)S(1)}, u32[]{:S(2)}, u32[]{:S(2)}) collective-permute-start(bf16[256,1024]{1,0:T(8,128)(2,1)S(1)} %copy-done), channel_id=1, source_target_pairs={{0,1},{1,0},{2,3},{3,2},{4,5},{5,4},{6,7},{7,6},{8,9},{9,8},{10,11... | collective-permute-start | bytes 1572872 | tf_op jit(solution)/shard_map/ppermute | solution.py:186
  49.8 50.2 %collective-permute-start.12 = (bf16[256,1024]{1,0:T(8,128)(2,1)S(1)}, bf16[256,1024]{1,0:T(8,128)(2,1)S(1)}, u32[]{:S(2)}, u32[]{:S(2)}) collective-permute-start(bf16[256,1024]{1,0:T(8,128)(2,1)S(1)} %get-tuple-element.39), channel_id=1, source_target_pairs={{0,64},{2,66},{4,68},{6,70},{8,72},{10,74},{12,76},{14,78},{16,80}... | collective-permute-start | bytes 1572872 | tf_op jit(solution)/shard_map/ppermute | solution.py:190
  56.8 40.3 %collective-permute-start.16 = (bf16[256,1024]{1,0:T(8,128)(2,1)S(1)}, bf16[256,1024]{1,0:T(8,128)(2,1)S(1)}, u32[]{:S(2)}, u32[]{:S(2)}) collective-permute-start(bf16[256,1024]{1,0:T(8,128)(2,1)S(1)} %get-tuple-element.44), channel_id=1, source_target_pairs={{0,1},{1,0},{2,3},{3,2},{4,5},{5,4},{6,7},{7,6},{8,9},{9,8},{10,11... | collective-permute-start | bytes 1572872 | tf_op jit(solution)/shard_map/ppermute | solution.py:186
  56.9 49.3 %collective-permute-start.18 = (bf16[256,1024]{1,0:T(8,128)(2,1)S(1)}, bf16[256,1024]{1,0:T(8,128)(2,1)S(1)}, u32[]{:S(2)}, u32[]{:S(2)}) collective-permute-start(bf16[256,1024]{1,0:T(8,128)(2,1)S(1)} %get-tuple-element.47), channel_id=1, source_target_pairs={{0,2},{4,6},{8,10},{12,14},{16,18},{20,22},{24,26},{28,30},{32,34}... | collective-permute-start | bytes 1572872 | tf_op jit(solution)/shard_map/ppermute | solution.py:192
  79.7 22.3 %collective-permute-start.11 = (bf16[256,1024]{1,0:T(8,128)(2,1)S(1)}, bf16[256,1024]{1,0:T(8,128)(2,1)S(1)}, u32[]{:S(2)}, u32[]{:S(2)}) collective-permute-start(bf16[256,1024]{1,0:T(8,128)(2,1)S(1)} %get-tuple-element.38), channel_id=1, source_target_pairs={{0,192},{2,194},{4,196},{6,198},{8,200},{10,202},{12,204},{14,206}... | collective-permute-start | bytes 1572872 | tf_op jit(solution)/shard_map/ppermute | solution.py:190
  82.0 25.9 %collective-permute-start.19 = (bf16[256,1024]{1,0:T(8,128)(2,1)S(1)}, bf16[256,1024]{1,0:T(8,128)(2,1)S(1)}, u32[]{:S(2)}, u32[]{:S(2)}) collective-permute-start(bf16[256,1024]{1,0:T(8,128)(2,1)S(1)} %get-tuple-element.49), channel_id=1, source_target_pairs={{2,4},{6,8},{10,12},{14,16},{18,20},{22,24},{26,28},{30,32},{34,36... | collective-permute-start | bytes 1572872 | tf_op jit(solution)/shard_map/ppermute | solution.py:192
  97.2 13.7 %collective-permute-start.17 = (bf16[256,1024]{1,0:T(8,128)(2,1)S(1)}, bf16[256,1024]{1,0:T(8,128)(2,1)S(1)}, u32[]{:S(2)}, u32[]{:S(2)}) collective-permute-start(bf16[256,1024]{1,0:T(8,128)(2,1)S(1)} %get-tuple-element.45), channel_id=1, source_target_pairs={{0,192},{2,194},{4,196},{6,198},{8,200},{10,202},{12,204},{14,206}... | collective-permute-start | bytes 1572872 | tf_op jit(solution)/shard_map/ppermute | solution.py:190
  100.0 14.5 %collective-permute-start.10 = (bf16[256,1024]{1,0:T(8,128)(2,1)S(1)}, bf16[256,1024]{1,0:T(8,128)(2,1)S(1)}, u32[]{:S(2)}, u32[]{:S(2)}) collective-permute-start(bf16[256,1024]{1,0:T(8,128)(2,1)S(1)} %get-tuple-element.35), channel_id=1, source_target_pairs={{0,64},{2,66},{4,68},{6,70},{8,72},{10,74},{12,76},{14,78},{16,80}... | collective-permute-start | bytes 1572872 | tf_op jit(solution)/shard_map/ppermute | solution.py:190
  102.0 20.3 %collective-permute-start.14 = (bf16[256,1024]{1,0:T(8,128)(2,1)S(1)}, bf16[256,1024]{1,0:T(8,128)(2,1)S(1)}, u32[]{:S(2)}, u32[]{:S(2)}) collective-permute-start(bf16[256,1024]{1,0:T(8,128)(2,1)S(1)} %get-tuple-element.41), channel_id=1, source_target_pairs={{2,4},{6,8},{10,12},{14,16},{18,20},{22,24},{26,28},{30,32},{34,36... | collective-permute-start | bytes 1572872 | tf_op jit(solution)/shard_map/ppermute | solution.py:192
  106.1 16.2 %collective-permute-start.15 = (bf16[256,1024]{1,0:T(8,128)(2,1)S(1)}, bf16[256,1024]{1,0:T(8,128)(2,1)S(1)}, u32[]{:S(2)}, u32[]{:S(2)}) collective-permute-start(bf16[256,1024]{1,0:T(8,128)(2,1)S(1)} %get-tuple-element.42), channel_id=1, source_target_pairs={{0,1},{1,0},{2,3},{3,2},{4,5},{5,4},{6,7},{7,6},{8,9},{9,8},{10,11... | collective-permute-start | bytes 1572872 | tf_op jit(solution)/shard_map/ppermute | solution.py:186
  107.9 14.4 %collective-permute-start.13 = (bf16[256,1024]{1,0:T(8,128)(2,1)S(1)}, bf16[256,1024]{1,0:T(8,128)(2,1)S(1)}, u32[]{:S(2)}, u32[]{:S(2)}) collective-permute-start(bf16[256,1024]{1,0:T(8,128)(2,1)S(1)} %get-tuple-element.40), channel_id=1, source_target_pairs={{0,2},{4,6},{8,10},{12,14},{16,18},{20,22},{24,26},{28,30},{32,34}... | collective-permute-start | bytes 1572872 | tf_op jit(solution)/shard_map/ppermute | solution.py:192
